TPU v7x, 768 devices: a whole 4x8x12 slice. The times are simulated.
768 devices in a mesh: row: 8 (over x, core), col: 12 (over z), state: 8 (over y).
Axes of the slice: x: 4, y: 8, z: 12, core: 2. Of those that a mesh axis runs over, the one named last changes fastest.
Arguments:
- vectors: bfloat16 [768, 4, 128, 128], P(('row', 'col')), may hold values from -6 to 6
- onsite: float32 [768, 128], P(('row', 'col'), 'state'), may hold values from 1 to 10
- k_tiles: bfloat16 [768, 16, 128, 128], P(('row', 'col'), 'state'), may hold values from -0.125 to 0.125
- s_tiles: bfloat16 [768, 16, 128, 128], P(('row', 'col'), 'state'), may hold values from -0.0625 to 0.0625
- columns: int32 [768, 16], P(('row', 'col')), may hold values from 0 to 767, as said below
- counts: int32 [768], P(('row', 'col')), may hold values from 2 to 16, as said below
Outputs:
- correction: float32 [768, 4, 128, 128], P(('row', 'col'), None, 'state')
- ritz: float32 [4], replicated
Inputs may be any that keep to these rules, and one draw needn't show every extreme that they name: `columns`: the screened blocks of block row i lie in block rows between the first block row of i's device minus 8 and its last block row plus 8, inside the grid; each row lists distinct blocks, its own block in slot 0. `counts`: some block row has all 16 slots live.
All inputs are finite; a program needn't handle non-finite values.
Results may differ from a plain program's by a relative error of at most 0.025.
Values may be sent and summed in bfloat16 or wider, within the bound.
No kernel may reach another device: no remote copies, remote signals or barrier semaphores. Data moves between devices by JAX's collectives and lax.ppermute only.
A program may use at most 32 MiB of HBM per device.

v0:
```python
import jax
import jax.numpy as jnp
from jax import lax
from jax.sharding import PartitionSpec as P

REACH = 8


def with_halo(block, sides, width):
    for axis, dim in sides:
        count = lax.axis_size(axis)
        forward = [(i, i + 1) for i in range(count - 1)]
        backward = [(target, source) for source, target in forward]
        low = lax.ppermute(
            lax.slice_in_dim(block, block.shape[dim] - width, None, axis=dim), axis, forward
        )
        high = lax.ppermute(lax.slice_in_dim(block, 0, width, axis=dim), axis, backward)
        block = jnp.concatenate([low, block, high], axis=dim)
    return block


def per_device(vectors, onsite, k_tiles, s_tiles, columns, counts):
    rows_blk = vectors.shape[0]
    states = vectors.shape[1]
    width = vectors.shape[2]
    layers = lax.axis_size("state")
    layer = lax.axis_index("state")
    own = width // layers
    device = lax.axis_index(("row", "col"))
    padded = with_halo(vectors, ((("row", "col"), 0),), REACH)
    local_cols = columns - (device * rows_blk - REACH)
    slot_ids = lax.broadcasted_iota(jnp.int32, columns.shape, 1)
    live_all = (slot_ids < counts[:, None]).astype(jnp.float32)

    def pick(slot):
        index = lax.dynamic_index_in_dim(local_cols, slot, 1, keepdims=False)
        gate = lax.dynamic_index_in_dim(live_all, slot, 1, keepdims=False)
        return (jnp.take(padded, index, axis=0), gate)

    slot_dev = k_tiles.shape[1]
    first = layer * slot_dev

    def step(slot, total):
        blocks, gate = pick(first + slot)
        k_rows = lax.dynamic_index_in_dim(k_tiles, slot, 1, keepdims=False)
        s_rows = lax.dynamic_index_in_dim(s_tiles, slot, 1, keepdims=False)
        k_part = jnp.einsum("rab,rsbc->arsc", k_rows, blocks, preferred_element_type=jnp.float32)
        s_part = jnp.einsum("rab,rsbc->arsc", s_rows, blocks, preferred_element_type=jnp.float32)
        weight = gate[None, None, :, None, None]
        return total + jnp.stack([k_part, s_part], axis=1) * weight

    start_total = jnp.zeros((own * lax.axis_size("state"), 2, rows_blk, states, width), jnp.float32)
    summed = lax.psum_scatter(
        lax.fori_loop(0, slot_dev, step, start_total), "state", scatter_dimension=0, tiled=True
    )
    products = jnp.transpose(summed, (1, 2, 3, 0, 4))
    mine = lax.dynamic_slice_in_dim(vectors, layer * own, own, 2).astype(jnp.float32)
    kx = onsite[:, None, :, None] * mine + products[0]
    sx = mine + products[1]
    cross_local = jnp.sum(sx * kx, axis=(0, 2, 3))
    power_local = jnp.sum(sx * sx, axis=(0, 2, 3))
    cross, power = lax.psum((cross_local, power_local), ("row", "col", "state"))
    ritz = cross / (power + 1e-06)
    resid = kx - ritz[None, :, None, None] * sx
    norm = lax.psum(jnp.sum(resid * resid, axis=(0, 2, 3)), ("row", "col", "state"))
    cells = lax.axis_size(("row", "col")) * rows_blk * width * width
    correction = resid * lax.rsqrt(norm / cells + 1e-06)[None, :, None, None]
    return (correction, ritz)


def solution(mesh):
    placed = (
        P(("row", "col"), None, None, None),
        P(("row", "col"), "state"),
        P(("row", "col"), "state", None, None),
        P(("row", "col"), "state", None, None),
        P(("row", "col"), None),
        P(("row", "col")),
    )
    return jax.shard_map(
        per_device,
        mesh=mesh,
        in_specs=placed,
        out_specs=(P(("row", "col"), None, "state", None), P()),
        check_vma=False,
    )
```

profile of v0, /device:TPU:1, one launch (start us, length us, event | category | flops | bytes accessed | tf_op | source)
XLA Modules:
  0.0 356.2 jit_solution(14242727001456735453)
XLA Ops:
  7.2 5.0 %collective-permute-start = (bf16[8,4,128,128]{3,2,1,0:T(8,128)(2,1)}, bf16[8,4,128,128]{3,2,1,0:T(8,128)(2,1)S(1)}, u32[]{:S(2)}, u32[]{:S(2)}) collective-permute-start(bf16[8,4,128,128]{3,2,1,0:T(8,128)(2,1)} %param.8), channel_id=1, source_target_pairs={{0,8},{8,16},{16,24},{24,32},{32,40},{40,48},{48,56},{56,64},{64,7... | collective-permute-start | bytes 3145736 | tf_op jit(solution)/shard_map/ppermute | solution.py:14
  12.2 12.8 %collective-permute-start.1 = (bf16[8,4,128,128]{3,2,1,0:T(8,128)(2,1)}, bf16[8,4,128,128]{3,2,1,0:T(8,128)(2,1)S(1)}, u32[]{:S(2)}, u32[]{:S(2)}) collective-permute-start(bf16[8,4,128,128]{3,2,1,0:T(8,128)(2,1)} %param.8), channel_id=1, source_target_pairs={{8,0},{16,8},{24,16},{32,24},{40,32},{48,40},{56,48},{64,56},{72,6... | collective-permute-start | bytes 3145736 | tf_op jit(solution)/shard_map/ppermute | solution.py:17
  25.0 0.8 copy.10
  25.8 0.7 fusion.11
  26.4 19.7 %collective-permute-done = bf16[8,4,128,128]{3,2,1,0:T(8,128)(2,1)S(1)} collective-permute-done((bf16[8,4,128,128]{3,2,1,0:T(8,128)(2,1)}, bf16[8,4,128,128]{3,2,1,0:T(8,128)(2,1)S(1)}, u32[]{:S(2)}, u32[]{:S(2)}) %collective-permute-start) | collective-permute-done | bytes 1048608 | tf_op jit(solution)/shard_map/ppermute | solution.py:14
  46.1 2.9 pad_maximum_fusion
  49.1 16.5 %while.14 = (s32[]{:T(128)}, f32[128,2,8,4,128]{0,4,3,2,1:T(8,128)}, s32[]{:T(128)}, s32[8,16]{0,1:T(8,128)S(1)}, bf16[24,4,128,128]{3,2,1,0:T(8,128)(2,1)}, /*i...) while((s32[]{:T(128)}, ...), condition=%wide.region_1.2_spmd.clone, body=%wide.region_0.1_spmd.clone.sunk | while | flops 273679424 | bytes 55055836 | solution.py:54
  49.1 2.6 gather_fusion
  52.3 0.6 convolution_bitcast_fusion.4
  52.9 1.0 copy-done
  53.9 1.5 fusion.19
  55.4 1.9 copy-done.1
  57.4 2.6 gather_fusion
  60.6 0.6 convolution_bitcast_fusion.4
  61.2 1.0 copy-done
  62.2 1.5 fusion.19
  63.7 1.9 copy-done.1
  65.6 5.4 %copy.13 = f32[128,2,8,4,128]{4,0,3,2,1:T(8,128)} copy(f32[128,2,8,4,128]{0,4,3,2,1:T(8,128)} %get-tuple-element.141) | data formatting | bytes 8388608 | tf_op jit(solution)/shard_map/while | solution.py:54
  71.0 60.7 %reduce-scatter.2.cloned.1.call-done = f32[16,2,8,4,128]{4,0,3,2,1:T(8,128)} async-done(((f32[128,2,8,4,128]{4,0,3,2,1:T(8,128)}), f32[16,2,8,4,128]{4,0,3,2,1:T(8,128)}) %reduce-scatter.2.cloned.1.call-update) | async-done | bytes 524304 | tf_op jit(solution)/shard_map/reduce_scatter | solution.py:53
  131.7 1.3 multiply_reduce_fusion.1
  133.0 110.6 %all-reduce = (f32[4]{0:T(128)S(1)}, f32[4]{0:T(128)S(1)}) all-reduce(f32[4]{0:T(128)S(1)} %get-tuple-element.178, f32[4]{0:T(128)S(1)} %get-tuple-element.177), channel_id=1, replica_groups=mesh['row'=8,'col'=12,'state'=8] {'row','col','state'}, use_global_device_ids=true, to_apply=%region_4.5 | all-reduce | flops 8 | bytes 64 | tf_op jit(solution)/shard_map/psum | solution.py:62
  243.5 1.3 multiply_reduce_fusion
  244.8 103.7 %psum.23 = f32[4]{0:T(128)S(1)} all-reduce(f32[4]{0:T(128)S(1)} %get-tuple-element.199), channel_id=1, replica_groups=mesh['row'=8,'col'=12,'state'=8] {'row','col','state'}, use_global_device_ids=true, to_apply=%region_8.9 | all-reduce | flops 4 | bytes 32 | tf_op jit(solution)/shard_map/psum | solution.py:65
  348.5 0.8 broadcast_multiply_fusion
  (27 shorter events, 1.3 us)
Async XLA Ops:
  7.2 41.9 %copy-start.3 = (bf16[8,2,128,128]{3,2,1,0:T(8,128)(2,1)S(1)}, bf16[8,2,128,128]{3,2,1,0:T(8,128)(2,1)}, u32[]{:S(2)}) copy-start(bf16[8,2,128,128]{3,2,1,0:T(8,128)(2,1)} %param.11) | copy-start | bytes 1572868
  7.2 41.9 %copy-start.2 = (bf16[8,2,128,128]{3,2,1,0:T(8,128)(2,1)S(1)}, bf16[8,2,128,128]{3,2,1,0:T(8,128)(2,1)}, u32[]{:S(2)}) copy-start(bf16[8,2,128,128]{3,2,1,0:T(8,128)(2,1)} %param.10) | copy-start | bytes 1572868
  7.2 124.5 %reduce-scatter.2.cloned.1.call-start = ((), (), s32[]{:S(2)}) async-start(), calls=%async_computation.1 | async-start | bytes 4718592 | tf_op jit(solution)/shard_map/reduce_scatter | solution.py:53
  7.2 38.9 %collective-permute-start = (bf16[8,4,128,128]{3,2,1,0:T(8,128)(2,1)}, bf16[8,4,128,128]{3,2,1,0:T(8,128)(2,1)S(1)}, u32[]{:S(2)}, u32[]{:S(2)}) collective-permute-start(bf16[8,4,128,128]{3,2,1,0:T(8,128)(2,1)} %param.8), channel_id=1, source_target_pairs={{0,8},{8,16},{16,24},{24,32},{32,40},{40,48},{48,56},{56,64},{64,7... | collective-permute-start | bytes 3145736 | tf_op jit(solution)/shard_map/ppermute | solution.py:14
  12.2 33.9 %collective-permute-start.1 = (bf16[8,4,128,128]{3,2,1,0:T(8,128)(2,1)}, bf16[8,4,128,128]{3,2,1,0:T(8,128)(2,1)S(1)}, u32[]{:S(2)}, u32[]{:S(2)}) collective-permute-start(bf16[8,4,128,128]{3,2,1,0:T(8,128)(2,1)} %param.8), channel_id=1, source_target_pairs={{8,0},{16,8},{24,16},{32,24},{40,32},{48,40},{56,48},{64,56},{72,6... | collective-permute-start | bytes 3145736 | tf_op jit(solution)/shard_map/ppermute | solution.py:17
  51.7 2.2 copy-start
  55.4 1.9 copy-start.1
  60.0 2.2 copy-start
  63.6 1.9 copy-start.1
  71.0 60.7 %copy-start.4 = (f32[8,16]{1,0:T(8,128)S(1)}, f32[8,16]{1,0:T(8,128)}, u32[]{:S(2)}) copy-start(f32[8,16]{1,0:T(8,128)} %param.9) | copy-start | bytes 1540
  243.5 105.8 %copy-start.5 = (f32[4]{0:T(128)}, f32[4]{0:T(128)S(1)}, u32[]{:S(2)}) copy-start(f32[4]{0:T(128)S(1)} %add_divide_fusion) | copy-start | bytes 52
Sparse Core Ops, SparseCore 0:
  71.1 60.5 reduce-scatter.1
where the time goes:
time: 357 us; the launch traced here: 356 us
  blocking collectives  214 us (60%)
  waiting for transfers between devices  80.4 us (23%)
  starting transfers between devices  17.8 us (5%)
  local copies, waits for them, and re-layouts  17.3 us (5%)
  between operations  14.1 us (4%)
  other arithmetic  9.93 us (3%)
    psum x1, blocking collectives, per_device(): cross, power = lax.psum((cross_local, power_local), ('row', 'col', 'state'))  111 us
    psum x1, blocking collectives, per_device(): lax.psum(jnp.sum(resid * resid, axis=(0, 2, 3)), ('row', 'col', 'state'))  104 us
    reduce_scatter x1, waiting for transfers between devices, per_device(): lax.psum_scatter(lax.fori_loop(0, slot_dev, step, start_total), 'state',...  60.7 us
    ppermute x1, waiting for transfers between devices, with_halo(): lax.ppermute(lax.slice_in_dim(block, block.shape[dim] - width, None, axis...  19.7 us
    ppermute x1, starting transfers between devices, with_halo(): lax.ppermute(lax.slice_in_dim(block, 0, width, axis=dim), axis, backward)  12.8 us
  transfers between devices with their start and end apart: 3, of which 2 were waited for; matrix products, arithmetic and copies ran while one was open for 0% of the time, Pallas kernels for 0%

commit v1 on v0

v1 whole, which is shorter than its diff:
```python
import functools

import jax
import jax.numpy as jnp
from jax import lax
from jax.experimental import pallas as pl
from jax.experimental.pallas import tpu as pltpu
from jax.sharding import PartitionSpec as P

REACH = 8
EPS = 1e-06
VMEM = pl.BlockSpec(memory_space=pltpu.VMEM)
SMEM = pl.BlockSpec(memory_space=pltpu.SMEM)
LIMIT = 48 * 1024 * 1024


def lanes(values, width=128):
    lane = lax.broadcasted_iota(jnp.int32, (1, width), 1)
    row = jnp.zeros((1, width), jnp.float32)
    for k, value in enumerate(values):
        row = jnp.where(lane == k, value, row)
    return row


def product_kernel(
    states, place_ref, layer_ref, tiles_ref, low_ref, mid_ref, high_ref, onsite_ref,
    kx_ref, sx_ref, stat_ref, oper_ref,
):
    layers, _, rows_blk, slot_dev, own, width = tiles_ref.shape
    half = rows_blk * own
    span = low_ref.shape[0] + mid_ref.shape[0] + high_ref.shape[0]
    oper_ref[:, : span * width] = jnp.zeros((2 * half, span * width), oper_ref.dtype)
    for i in range(rows_blk):
        for y in range(layers):
            for m in range(slot_dev):
                at = pl.ds(pl.multiple_of(place_ref[i, y * slot_dev + m] * width, width), width)
                for op in range(2):
                    first = op * half + i * own
                    oper_ref[first : first + own, at] = tiles_ref[y, op, i, m]

    mine_at = pl.ds(pl.multiple_of(layer_ref[0] * own, own), own)
    diagonal = onsite_ref[...].reshape(half, width)
    power, cross, norm = [], [], []
    for s in range(0, states, 2):
        total = jnp.zeros((2 * half, 2 * width), jnp.float32)
        at = 0
        for ref in (low_ref, mid_ref, high_ref):
            depth = ref.shape[0] * width
            blocks = jnp.concatenate(
                [ref[:, t].reshape(depth, width) for t in (s, s + 1)], axis=1
            )
            total = total + jnp.dot(
                oper_ref[:, at : at + depth], blocks, preferred_element_type=jnp.float32
            )
            at += depth
        for t in range(2):
            mine = mid_ref[:, s + t, mine_at, :].astype(jnp.float32).reshape(half, width)
            coupled = total[:half, t * width : (t + 1) * width]
            intersected = total[half:, t * width : (t + 1) * width]
            kx = diagonal * mine + coupled
            sx = mine + intersected
            kx_ref[:, s + t] = kx.reshape(rows_blk, own, width)
            sx_ref[:, s + t] = sx.reshape(rows_blk, own, width)
            p = jnp.sum(sx * sx, keepdims=True)
            c = jnp.sum(sx * kx, keepdims=True)
            resid = kx - (c / (p + EPS)) * sx
            power.append(p)
            cross.append(c)
            norm.append(jnp.sum(resid * resid, keepdims=True))
    stat_ref[...] = jnp.broadcast_to(lanes(power + cross + norm)[None], stat_ref.shape)


def merged(parts, states):
    power = parts
    cross = pltpu.roll(parts, parts.shape[1] - states, 1)
    norm = pltpu.roll(parts, parts.shape[1] - 2 * states, 1)
    power_all = jnp.sum(power, axis=0, keepdims=True)
    cross_all = jnp.sum(cross, axis=0, keepdims=True)
    ratio = cross / (power + EPS)
    ritz = cross_all / (power_all + EPS)
    gap = ratio - ritz
    norm_all = jnp.sum(norm + (2 * EPS) * gap * ratio + gap * gap * power, axis=0, keepdims=True)
    return power_all, cross_all, norm_all, ritz


def pick(row, k):
    return row[:, k : k + 1]


def merge_kernel(states, parts_ref, stat_ref):
    power, cross, norm, _ = merged(parts_ref[...].reshape(parts_ref.shape[0], -1), states)
    row = lanes([pick(a, k) for a in (power, cross, norm) for k in range(states)])
    stat_ref[...] = jnp.broadcast_to(row[None], stat_ref.shape)


def final_kernel(states, cells, parts_ref, kx_ref, sx_ref, out_ref, ritz_ref):
    _, _, norm, ritz = merged(parts_ref[...].reshape(parts_ref.shape[0], -1), states)
    scale = lax.rsqrt(norm / cells + EPS)
    for s in range(states):
        out_ref[:, s] = (kx_ref[:, s] - pick(ritz, s)[None] * sx_ref[:, s]) * pick(scale, s)[None]
    ritz_ref[...] = ritz


def per_device(vectors, onsite, k_tiles, s_tiles, columns, counts):
    rows_blk, states, width, _ = vectors.shape
    layers = lax.axis_size("state")
    layer = lax.axis_index("state")
    own = width // layers
    slot_dev = k_tiles.shape[1]
    device = lax.axis_index(("row", "col"))
    span = rows_blk + 2 * REACH

    count = lax.axis_size(("row", "col"))
    forward = [(i, i + 1) for i in range(count - 1)]
    backward = [(b, a) for a, b in forward]
    low = lax.ppermute(vectors[rows_blk - REACH :], ("row", "col"), forward)
    high = lax.ppermute(vectors[:REACH], ("row", "col"), backward)

    tiles = jnp.stack([k_tiles, s_tiles]).reshape(2, rows_blk, slot_dev, layers, own, width)
    tiles = jnp.transpose(tiles, (3, 0, 1, 2, 4, 5))
    tiles = lax.all_to_all(tiles, "state", 0, 0, tiled=True)

    slot_ids = lax.broadcasted_iota(jnp.int32, columns.shape, 1)
    place = jnp.where(slot_ids < counts[:, None], columns - (device * rows_blk - REACH), span)
    place = jnp.clip(place, 0, span)
    diagonal = jnp.broadcast_to(onsite[:, :, None], (rows_blk, own, width))

    inner = lax.axis_size(("row", "state"))
    outer = lax.axis_size("col")
    outs = jax.ShapeDtypeStruct((rows_blk, states, own, width), jnp.float32)
    params = pltpu.CompilerParams(vmem_limit_bytes=LIMIT)
    kx, sx, stat = pl.pallas_call(
        functools.partial(product_kernel, states),
        out_shape=(outs, outs, jax.ShapeDtypeStruct((inner, 1, width), jnp.float32)),
        in_specs=[SMEM, SMEM] + [VMEM] * 5,
        out_specs=(VMEM, VMEM, VMEM),
        scratch_shapes=[pltpu.VMEM((2 * rows_blk * own, (span + 1) * width), jnp.bfloat16)],
        compiler_params=params,
    )(place, layer.reshape(1), tiles, low, vectors, high, diagonal)

    stat = lax.all_to_all(stat, ("row", "state"), 0, 0, tiled=True)
    stat = pl.pallas_call(
        functools.partial(merge_kernel, states),
        out_shape=jax.ShapeDtypeStruct((outer, 1, width), jnp.float32),
        in_specs=[VMEM],
        out_specs=VMEM,
    )(stat)
    stat = lax.all_to_all(stat, "col", 0, 0, tiled=True)
    correction, ritz = pl.pallas_call(
        functools.partial(final_kernel, states, count * rows_blk * width * width),
        out_shape=(outs, jax.ShapeDtypeStruct((1, width), jnp.float32)),
        in_specs=[VMEM] * 3,
        out_specs=(VMEM, VMEM),
    )(stat, kx, sx)
    return correction, ritz[0, :states]


def solution(mesh):
    placed = (
        P(("row", "col"), None, None, None),
        P(("row", "col"), "state"),
        P(("row", "col"), "state", None, None),
        P(("row", "col"), "state", None, None),
        P(("row", "col"), None),
        P(("row", "col")),
    )
    return jax.shard_map(
        per_device,
        mesh=mesh,
        in_specs=placed,
        out_specs=(P(("row", "col"), None, "state", None), P()),
        check_vma=False,
    )
```

time: 357 us -> 95.4 us (0.27)
  blocking collectives: 214 us -> 36.7 us
  waiting for transfers between devices: 80.4 us -> 19.9 us
  local copies, waits for them, and re-layouts: 17.3 us -> 3.33 us
  between operations: 14.1 us -> 0.71 us
  other arithmetic: 9.93 us -> 2.51 us
  starting transfers between devices: 17.8 us -> 24.9 us
  Pallas kernels: 0 us -> 6.72 us
    psum x2 -> x0, blocking collectives: 214 us -> none  [the longest x1 111 us: per_device(): cross, power = lax.psum((cross_local, power_local), ('row', 'col', 'state'))]
    reduce_scatter x1 -> x0, waiting for transfers between devices: 60.7 us -> none  [per_device(): lax.psum_scatter(lax.fori_loop(0, slot_dev, step, start_total), 'state',...]
    all_to_all x0 -> x2, blocking collectives: none -> 36.7 us  [the longest x1 21.1 us: per_device(): stat = lax.all_to_all(stat, ('row', 'state'), 0, 0, tiled=True)]
    while x9 -> x0, local copies, waits for them, and re-layouts: 11.3 us -> none
    all_to_all x0 -> x1, starting transfers between devices: none -> 7.78 us  [per_device(): tiles = lax.all_to_all(tiles, 'state', 0, 0, tiled=True)]
    pallas_call x0 -> x3, Pallas kernels: none -> 6.72 us  [the longest x1 3.22 us: per_device(): pl.pallas_call(functools.partial(product_kernel, states), out_shape=(outs...]
    gather x2 -> x0, local copies, waits for them, and re-layouts: 5.28 us -> none  [pick(): return (jnp.take(padded, index, axis=0), gate)]
  transfers between devices with their start and end apart: 3 -> 3, of which waited for: 2 -> 1; matrix products, arithmetic and copies ran while one was open for 0% -> 0% of each run, Pallas kernels for 0% -> 0%
where the time goes in v1:
time: 95.4 us; the launch traced here: 94.7 us
  blocking collectives  36.7 us (38%)
  starting transfers between devices  24.9 us (26%)
  waiting for transfers between devices  19.9 us (21%)
  Pallas kernels  6.72 us (7%)
  local copies, waits for them, and re-layouts  3.33 us (3%)
  other arithmetic  2.51 us (3%)
    all_to_all x1, blocking collectives, per_device(): stat = lax.all_to_all(stat, ('row', 'state'), 0, 0, tiled=True)  21.1 us
    ppermute x1, waiting for transfers between devices, per_device(): low = lax.ppermute(vectors[rows_blk - REACH:], ('row', 'col'), forward)  19.9 us
    all_to_all x1, blocking collectives, per_device(): stat = lax.all_to_all(stat, 'col', 0, 0, tiled=True)  15.6 us
    ppermute x1, starting transfers between devices, per_device(): high = lax.ppermute(vectors[:REACH], ('row', 'col'), backward)  13.1 us
    all_to_all x1, starting transfers between devices, per_device(): tiles = lax.all_to_all(tiles, 'state', 0, 0, tiled=True)  7.78 us
    ppermute x1, starting transfers between devices, per_device(): low = lax.ppermute(vectors[rows_blk - REACH:], ('row', 'col'), forward)  4 us
    pallas_call x1, Pallas kernels, per_device(): pl.pallas_call(functools.partial(product_kernel, states), out_shape=(outs...  3.22 us
    unnamed x14, local copies, waits for them, and re-layouts  2.75 us
  transfers between devices with their start and end apart: 3, of which 1 were waited for; matrix products, arithmetic and copies ran while one was open for 0% of the time, Pallas kernels for 0%

profile of v1, /device:TPU:1, one launch (start us, length us, event | category | flops | bytes accessed | tf_op | source)
XLA Modules:
  0.0 94.7 jit_solution(15447602433451166029)
XLA Ops:
  0.6 2.4 %copy_bitcast_fusion = bf16[8,2,8,2,16,128]{5,4,3,2,1,0:T(8,128)(2,1)} fusion(bf16[1,8,2,8,16,128]{5,4,3,2,1,0:T(8,128)(2,1)} %bitcast.7, bf16[1,8,2,8,16,128]{5,4,3,2,1,0:T(8,128)(2,1)} %bitcast.8), kind=kLoop, calls=%fused_computation.1 | loop fusion | flops 524288 | bytes 2097152 | tf_op jit(solution)/shard_map/transpose | solution.py:120
  3.1 7.8 %all-to-all-start = ((bf16[8,2,8,2,16,128]{5,4,3,2,1,0:T(8,128)(2,1)}), bf16[8,2,8,2,16,128]{5,4,3,2,1,0:T(8,128)(2,1)S(1)}, u32[]{:S(2)}, u32[]{:S(2)}) async-start(bf16[8,2,8,2,16,128]{5,4,3,2,1,0:T(8,128)(2,1)} %copy_bitcast_fusion), calls=%async_computation | async-start | bytes 2097152 | tf_op jit(solution)/shard_map/all_to_all | solution.py:121
  10.9 0.0 copy-done
  10.9 4.0 %collective-permute-start = (bf16[8,4,128,128]{3,2,1,0:T(8,128)(2,1)S(1)}, bf16[8,4,128,128]{3,2,1,0:T(8,128)(2,1)S(1)}, u32[]{:S(2)}, u32[]{:S(2)}) collective-permute-start(bf16[8,4,128,128]{3,2,1,0:T(8,128)(2,1)S(1)} %copy-done), channel_id=1, source_target_pairs={{0,8},{8,16},{16,24},{24,32},{32,40},{40,48},{48,56},{56,64},{64,7... | collective-permute-start | bytes 3145736 | tf_op jit(solution)/shard_map/ppermute | solution.py:116
  14.9 13.1 %collective-permute-start.1 = (bf16[8,4,128,128]{3,2,1,0:T(8,128)(2,1)S(1)}, bf16[8,4,128,128]{3,2,1,0:T(8,128)(2,1)}, u32[]{:S(2)}, u32[]{:S(2)}) collective-permute-start(bf16[8,4,128,128]{3,2,1,0:T(8,128)(2,1)S(1)} %copy-done), channel_id=1, source_target_pairs={{8,0},{16,8},{24,16},{32,24},{40,32},{48,40},{56,48},{64,56},{72,6... | collective-permute-start | bytes 3145736 | tf_op jit(solution)/shard_map/ppermute | solution.py:117
  28.0 0.0 copy-start.4
  28.0 0.0 copy-start.5
  28.0 0.7 copy-done.4
  28.6 0.0 copy-done.5
  28.6 0.1 select_clamp_fusion.place_ref
  28.7 19.9 %collective-permute-done.low_ref = bf16[8,4,128,128]{3,2,1,0:T(8,128)(2,1)S(1)} collective-permute-done((bf16[8,4,128,128]{3,2,1,0:T(8,128)(2,1)S(1)}, bf16[8,4,128,128]{3,2,1,0:T(8,128)(2,1)S(1)}, u32[]{:S(2)}, u32[]{:S(2)}) %collective-permute-start) | collective-permute-done | bytes 1048608 | tf_op jit(solution)/shard_map/ppermute | solution.py:116
  48.6 0.0 collective-permute-done.1.high_ref
  48.6 0.0 all-to-all-done.tiles_ref
  48.6 0.0 copy-done.3
  48.6 0.1 broadcast_in_dim.4.onsite_ref
  48.7 3.2 %shard_map.77 = (f32[8,4,16,128]{3,2,1,0:T(8,128)S(1)}, f32[8,4,16,128]{3,2,1,0:T(8,128)S(1)}, f32[64,1,128]{2,1,0:T(1,128)S(1)}) custom-call(s32[8,16]{1,0:T(8,128)S(1)} %select_clamp_fusion.place_ref, s32[1]{0:T(128)} %bitcast.layer_ref, bf16[8,2,8,2,16,128]{5,4,3,2,1,0:T(8,128)(2,1)S(1)} %all-to-all-done.tiles_ref, ...), custom_call_target="tpu_custom_call" | custom-call | tf_op jit(solution)/shard_map/pallas_call | solution.py:132
  51.9 0.7 copy-done.1
  52.6 0.7 copy-done.2
  53.3 21.1 %all_to_all.15.parts_ref = f32[64,1,128]{2,1,0:T(1,128)} all-to-all(f32[64,1,128]{2,1,0:T(1,128)S(1)} %get-tuple-element.7), channel_id=1, replica_groups=mesh['row'=8,'col'=12,'state'=8] {'row','state'}, dimensions={0} | all-to-all | bytes 65536 | tf_op jit(solution)/shard_map/all_to_all | solution.py:141
  74.4 1.6 %shard_map.78 = f32[12,1,128]{2,1,0:T(1,128)} custom-call(f32[64,1,128]{2,1,0:T(1,128)} %all_to_all.15.parts_ref), custom_call_target="tpu_custom_call" | custom-call | tf_op jit(solution)/shard_map/pallas_call | solution.py:142
  75.9 15.6 %all_to_all.16.parts_ref = f32[12,1,128]{2,1,0:T(1,128)} all-to-all(f32[12,1,128]{2,1,0:T(1,128)} %shard_map.78), channel_id=1, replica_groups=mesh['row'=8,'col'=12,'state'=8] {'col'}, dimensions={0} | all-to-all | bytes 12288 | tf_op jit(solution)/shard_map/all_to_all | solution.py:148
  91.6 1.9 %shard_map.79 = (f32[8,4,16,128]{3,2,1,0:T(8,128)}, f32[1,128]{1,0:T(1,128)}) custom-call(f32[12,1,128]{2,1,0:T(1,128)} %all_to_all.16.parts_ref, f32[8,4,16,128]{3,2,1,0:T(8,128)} %copy-done.1, f32[8,4,16,128]{3,2,1,0:T(8,128)} %copy-done.2), custom_call_target="tpu_custom_call" | custom-call | tf_op jit(solution)/shard_map/pallas_call | solution.py:149
  93.5 0.7 copy-done.6
  94.2 0.5 slice_bitcast_fusion
  (5 shorter events, 0.0 us)
Async XLA Ops:
  3.1 7.8 %copy-start = (bf16[8,4,128,128]{3,2,1,0:T(8,128)(2,1)S(1)}, bf16[8,4,128,128]{3,2,1,0:T(8,128)(2,1)}, u32[]{:S(2)}) copy-start(bf16[8,4,128,128]{3,2,1,0:T(8,128)(2,1)} %mid_ref.1) | copy-start | bytes 3145732
  3.1 45.5 %all-to-all-start = ((bf16[8,2,8,2,16,128]{5,4,3,2,1,0:T(8,128)(2,1)}), bf16[8,2,8,2,16,128]{5,4,3,2,1,0:T(8,128)(2,1)S(1)}, u32[]{:S(2)}, u32[]{:S(2)}) async-start(bf16[8,2,8,2,16,128]{5,4,3,2,1,0:T(8,128)(2,1)} %copy_bitcast_fusion), calls=%async_computation | async-start | bytes 2097152 | tf_op jit(solution)/shard_map/all_to_all | solution.py:121
  10.9 37.7 %collective-permute-start = (bf16[8,4,128,128]{3,2,1,0:T(8,128)(2,1)S(1)}, bf16[8,4,128,128]{3,2,1,0:T(8,128)(2,1)S(1)}, u32[]{:S(2)}, u32[]{:S(2)}) collective-permute-start(bf16[8,4,128,128]{3,2,1,0:T(8,128)(2,1)S(1)} %copy-done), channel_id=1, source_target_pairs={{0,8},{8,16},{16,24},{24,32},{32,40},{40,48},{48,56},{56,64},{64,7... | collective-permute-start | bytes 3145736 | tf_op jit(solution)/shard_map/ppermute | solution.py:116
  14.9 33.7 %collective-permute-start.1 = (bf16[8,4,128,128]{3,2,1,0:T(8,128)(2,1)S(1)}, bf16[8,4,128,128]{3,2,1,0:T(8,128)(2,1)}, u32[]{:S(2)}, u32[]{:S(2)}) collective-permute-start(bf16[8,4,128,128]{3,2,1,0:T(8,128)(2,1)S(1)} %copy-done), channel_id=1, source_target_pairs={{8,0},{16,8},{24,16},{32,24},{40,32},{48,40},{56,48},{64,56},{72,6... | collective-permute-start | bytes 3145736 | tf_op jit(solution)/shard_map/ppermute | solution.py:117
  28.0 0.7 copy-start.4
  28.0 0.7 copy-start.5
  28.6 19.9 %copy-start.3 = (f32[8,16]{1,0:T(8,128)S(1)}, f32[8,16]{1,0:T(8,128)}, u32[]{:S(2)}) copy-start(f32[8,16]{1,0:T(8,128)} %param.7) | copy-start | bytes 1540
  51.9 0.7 copy-start.1
  52.6 0.7 copy-start.2
  93.5 0.7 copy-start.6

commit v2 on v1

v2 whole, which is shorter than its diff:
```python
import functools

import jax
import jax.numpy as jnp
from jax import lax
from jax.experimental import pallas as pl
from jax.experimental.pallas import tpu as pltpu
from jax.sharding import PartitionSpec as P

REACH = 8
EPS = 1e-06
MIB = 1024 * 1024
VMEM = pl.BlockSpec(memory_space=pltpu.VMEM)
SMEM = pl.BlockSpec(memory_space=pltpu.SMEM)
ANY = pl.BlockSpec(memory_space=pl.ANY)


def limit(mib):
    return pltpu.CompilerParams(vmem_limit_bytes=mib * MIB)


def lanes(values, width=128):
    lane = lax.broadcasted_iota(jnp.int32, (1, width), 1)
    row = jnp.zeros((1, width), jnp.float32)
    for k, value in enumerate(values):
        row = jnp.where(lane == k, value, row)
    return row


def send_kernel(k_ref, s_ref, out_ref, held_ref, in_sems, out_sems):
    layers, _, _, _, own, _ = out_ref.shape
    pairs = [(d, op) for d in range(layers) for op in range(2)]
    loads = []
    for d, op in pairs:
        part = (k_ref, s_ref)[op].at[:, :, pl.ds(d * own, own), :]
        loads.append(pltpu.make_async_copy(part, held_ref.at[d, op], in_sems.at[d, op]))
        loads[-1].start()
    stores = []
    for (d, op), load in zip(pairs, loads):
        load.wait()
        stores.append(
            pltpu.make_async_copy(held_ref.at[d, op], out_ref.at[d, op], out_sems.at[d, op])
        )
        stores[-1].start()
    for store in stores:
        store.wait()


def merged(power, cross, norm):
    power_all = jnp.sum(power, axis=0, keepdims=True)
    cross_all = jnp.sum(cross, axis=0, keepdims=True)
    ratio = cross / (power + EPS)
    ritz = cross_all / (power_all + EPS)
    gap = ratio - ritz
    norm_all = jnp.sum(norm + (2 * EPS) * gap * ratio + gap * gap * power, axis=0, keepdims=True)
    return power_all, cross_all, norm_all, ritz


def merged_rows(parts, states):
    width = parts.shape[1]
    cross = pltpu.roll(parts, width - states, 1)
    norm = pltpu.roll(parts, width - 2 * states, 1)
    return merged(parts, cross, norm)


def pick(row, k):
    return row[:, k : k + 1]


def packed(power, cross, norm, states):
    return lanes([pick(a, k) for a in (power, cross, norm) for k in range(states)])


def early_kernel(
    states, spot_ref, columns_ref, counts_ref, tiles_ref, low_ref, mid_ref, onsite_ref, total_ref, oper_ref
):
    layers, _, rows, slot_dev, own, width = tiles_ref.shape
    half = rows * own
    window = oper_ref.shape[1] // width - 1
    oper_ref[:, : window * width] = jnp.zeros((2 * half, window * width), oper_ref.dtype)
    for i in range(rows):
        for y in range(layers):
            for m in range(slot_dev):
                slot = y * slot_dev + m
                block = columns_ref[i, slot] - spot_ref[0]
                block = jnp.where(slot < counts_ref[i], block, window)
                block = jnp.clip(block, 0, window)
                at = pl.ds(pl.multiple_of(block * width, width), width)
                for op in range(2):
                    top = op * half + i * own
                    oper_ref[top : top + own, at] = tiles_ref[y, op, i, m]

    square = (own, own)
    eye = lax.broadcasted_iota(jnp.int32, square, 0) == lax.broadcasted_iota(jnp.int32, square, 1)
    diagonal = []
    for i in range(rows):
        terms = jnp.where(eye, jnp.broadcast_to(onsite_ref[i : i + 1, :], square), 0.0)
        diagonal.append(jnp.broadcast_to(jnp.sum(terms, axis=1, keepdims=True), (own, width)))
    diagonal = jnp.concatenate(diagonal, axis=0)
    mine_at = pl.ds(pl.multiple_of(spot_ref[1] * own, own), own)
    for s in range(0, states, 2):
        mine = jnp.concatenate(
            [mid_ref[:, t, mine_at, :].astype(jnp.float32).reshape(half, width) for t in (s, s + 1)],
            axis=1,
        )
        both = jnp.concatenate([diagonal, diagonal], axis=1)
        total = jnp.concatenate([both * mine, mine], axis=0)
        at = 0
        for ref in (low_ref, mid_ref):
            total = total + product(oper_ref, at, ref, s)
            at += ref.shape[0] * width
        total_ref[:, s * width : (s + 2) * width] = total


def product(oper_ref, at, blocks_ref, s):
    width = blocks_ref.shape[-1]
    depth = blocks_ref.shape[0] * width
    blocks = jnp.concatenate(
        [blocks_ref[:, t].reshape(depth, width) for t in (s, s + 1)], axis=1
    )
    return jnp.dot(oper_ref[:, at : at + depth], blocks, preferred_element_type=jnp.float32)


def late_kernel(states, total_ref, oper_ref, high_ref, kx_ref, sx_ref, stat_ref):
    rows, _, own, width = kx_ref.shape
    half = rows * own
    at = oper_ref.shape[1] - (high_ref.shape[0] + 1) * width
    power, cross, norm = [], [], []
    for s in range(0, states, 2):
        total = total_ref[:, s * width : (s + 2) * width] + product(oper_ref, at, high_ref, s)
        for t in range(2):
            kx = total[:half, t * width : (t + 1) * width]
            sx = total[half:, t * width : (t + 1) * width]
            kx_ref[:, s + t] = kx.reshape(rows, own, width)
            sx_ref[:, s + t] = sx.reshape(rows, own, width)
            p = jnp.sum(sx * sx, keepdims=True)
            c = jnp.sum(sx * kx, keepdims=True)
            resid = kx - (c / (p + EPS)) * sx
            power.append(p)
            cross.append(c)
            norm.append(jnp.sum(resid * resid, keepdims=True))
    row = lanes(power + cross + norm)
    stat_ref[...] = jnp.broadcast_to(row[None], stat_ref.shape)


def merge_kernel(states, parts_ref, stat_ref):
    power, cross, norm, _ = merged_rows(parts_ref[...].reshape(parts_ref.shape[0], -1), states)
    stat_ref[...] = jnp.broadcast_to(packed(power, cross, norm, states)[None], stat_ref.shape)


def final_kernel(states, cells, parts_ref, kx_ref, sx_ref, out_ref, ritz_ref):
    _, _, norm, ritz = merged_rows(parts_ref[...].reshape(parts_ref.shape[0], -1), states)
    scale = lax.rsqrt(norm / cells + EPS)
    for s in range(states):
        out_ref[:, s] = (kx_ref[:, s] - pick(ritz, s)[None] * sx_ref[:, s]) * pick(scale, s)[None]
        ritz_ref[s] = ritz[0, s]


def per_device(vectors, onsite, k_tiles, s_tiles, columns, counts):
    rows_blk, states, width, _ = vectors.shape
    layers = lax.axis_size("state")
    layer = lax.axis_index("state")
    own = width // layers
    slot_dev = k_tiles.shape[1]
    device = lax.axis_index(("row", "col"))
    window = rows_blk + 2 * REACH

    count = lax.axis_size(("row", "col"))
    forward = [(i, i + 1) for i in range(count - 1)]
    backward = [(b, a) for a, b in forward]
    low = lax.ppermute(vectors[rows_blk - REACH :], ("row", "col"), forward)
    high = lax.ppermute(vectors[:REACH], ("row", "col"), backward)

    send = pl.pallas_call(
        send_kernel,
        out_shape=jax.ShapeDtypeStruct((layers, 2, rows_blk, slot_dev, own, width), k_tiles.dtype),
        in_specs=[ANY, ANY],
        out_specs=ANY,
        scratch_shapes=[
            pltpu.VMEM((layers, 2, rows_blk, slot_dev, own, width), k_tiles.dtype),
            pltpu.SemaphoreType.DMA((layers, 2)),
            pltpu.SemaphoreType.DMA((layers, 2)),
        ],
        compiler_params=limit(8),
    )(*(pltpu.with_memory_space_constraint(t, pltpu.HBM) for t in (k_tiles, s_tiles)))
    tiles = lax.all_to_all(send, "state", 0, 0, tiled=True)

    spot = jnp.stack([device * rows_blk - REACH, layer])
    tall = 2 * rows_blk * own
    total, oper = pl.pallas_call(
        functools.partial(early_kernel, states),
        out_shape=(
            jax.ShapeDtypeStruct((tall, states * width), jnp.float32),
            jax.ShapeDtypeStruct((tall, (window + 1) * width), vectors.dtype),
        ),
        in_specs=[SMEM] * 3 + [VMEM] * 4,
        out_specs=(VMEM, VMEM),
        compiler_params=limit(12),
    )(spot, columns, counts, tiles, low, vectors, onsite)

    inner = lax.axis_size(("row", "state"))
    outer = lax.axis_size("col")
    outs = jax.ShapeDtypeStruct((rows_blk, states, own, width), jnp.float32)
    kx, sx, stat = pl.pallas_call(
        functools.partial(late_kernel, states),
        out_shape=(outs, outs, jax.ShapeDtypeStruct((inner, 1, width), jnp.float32)),
        in_specs=[VMEM] * 3,
        out_specs=(VMEM, VMEM, VMEM),
        compiler_params=limit(12),
    )(total, oper, high)

    stat = lax.all_to_all(stat, ("row", "state"), 0, 0, tiled=True)
    stat = pl.pallas_call(
        functools.partial(merge_kernel, states),
        out_shape=jax.ShapeDtypeStruct((outer, 1, width), jnp.float32),
        in_specs=[VMEM],
        out_specs=VMEM,
        compiler_params=limit(2),
    )(stat)
    stat = lax.all_to_all(stat, "col", 0, 0, tiled=True)
    correction, ritz = pl.pallas_call(
        functools.partial(final_kernel, states, count * rows_blk * width * width),
        out_shape=(outs, jax.ShapeDtypeStruct((states,), jnp.float32)),
        in_specs=[VMEM] * 3,
        out_specs=(VMEM, SMEM),
        compiler_params=limit(4),
    )(stat, kx, sx)
    return correction, ritz


def solution(mesh):
    placed = (
        P(("row", "col"), None, None, None),
        P(("row", "col"), "state"),
        P(("row", "col"), "state", None, None),
        P(("row", "col"), "state", None, None),
        P(("row", "col"), None),
        P(("row", "col")),
    )
    return jax.shard_map(
        per_device,
        mesh=mesh,
        in_specs=placed,
        out_specs=(P(("row", "col"), None, "state", None), P()),
        check_vma=False,
    )
```

time: 95.4 us -> 87.5 us (0.917)
  local copies, waits for them, and re-layouts: 3.33 us -> 0.02 us
  blocking collectives: 36.7 us -> 34 us
  other arithmetic: 2.51 us -> 0.08 us
    unnamed x14 -> x8, local copies, waits for them, and re-layouts: 2.75 us -> 0.02 us
    pallas_call x1 -> x3, Pallas kernels: 3.22 us -> 5.8 us  [the longest x1 2.4 us: per_device(): pl.pallas_call(functools.partial(early_kernel, states), out_shape=(jax.Sh...]
    transpose x1 -> x0, other arithmetic: 2.44 us -> none  [per_device(): tiles = jnp.transpose(tiles, (3, 0, 1, 2, 4, 5))]
    all_to_all x1, blocking collectives: 21.1 us -> 19.1 us  [per_device(): stat = lax.all_to_all(stat, ('row', 'state'), 0, 0, tiled=True)]
    pallas_call x1, Pallas kernels: 1.55 us -> 0.2 us  [per_device(): pl.pallas_call(functools.partial(merge_kernel, states), out_shape=jax.Sha...]
    pallas_call x1, Pallas kernels: 1.95 us -> 0.92 us  [per_device(): pl.pallas_call(functools.partial(final_kernel, states, count * rows_blk *...]
  transfers between devices with their start and end apart: 3 -> 3, of which waited for: 1 -> 1; matrix products, arithmetic and copies ran while one was open for 0% -> 0% of each run, Pallas kernels for 0% -> 3%
where the time goes in v2:
time: 87.5 us; the launch traced here: 87.2 us
  blocking collectives  34 us (39%)
  starting transfers between devices  24.7 us (28%)
  waiting for transfers between devices  20.7 us (24%)
  Pallas kernels  6.91 us (8%)
    ppermute x1, waiting for transfers between devices, per_device(): low = lax.ppermute(vectors[rows_blk - REACH:], ('row', 'col'), forward)  20.7 us
    all_to_all x1, blocking collectives, per_device(): stat = lax.all_to_all(stat, ('row', 'state'), 0, 0, tiled=True)  19.1 us
    all_to_all x1, blocking collectives, per_device(): stat = lax.all_to_all(stat, 'col', 0, 0, tiled=True)  15 us
    ppermute x1, starting transfers between devices, per_device(): high = lax.ppermute(vectors[:REACH], ('row', 'col'), backward)  13.1 us
    all_to_all x1, starting transfers between devices, per_device(): tiles = lax.all_to_all(send, 'state', 0, 0, tiled=True)  7.66 us
    ppermute x1, starting transfers between devices, per_device(): low = lax.ppermute(vectors[rows_blk - REACH:], ('row', 'col'), forward)  4 us
    pallas_call x1, Pallas kernels, per_device(): pl.pallas_call(functools.partial(early_kernel, states), out_shape=(jax.Sh...  2.4 us
    pallas_call x1, Pallas kernels, per_device(): pl.pallas_call(send_kernel, out_shape=jax.ShapeDtypeStruct((layers, 2, ro...  2.24 us
  transfers between devices with their start and end apart: 3, of which 1 were waited for; matrix products, arithmetic and copies ran while one was open for 0% of the time, Pallas kernels for 3%

profile of v2, /device:TPU:1, one launch (start us, length us, event | category | flops | bytes accessed | tf_op | source)
XLA Modules:
  0.0 87.2 jit_solution(12588849233353490925)
XLA Ops:
  0.6 0.0 copy-start
  0.6 0.0 copy-start.3
  0.7 0.0 copy-start.1
  0.7 0.0 copy-start.2
  0.7 2.2 %shard_map.77 = bf16[8,2,8,2,16,128]{5,4,3,2,1,0:T(8,128)(2,1)} custom-call(bf16[8,2,128,128]{3,2,1,0:T(8,128)(2,1)} %k_ref.1, bf16[8,2,128,128]{3,2,1,0:T(8,128)(2,1)} %s_ref.1), custom_call_target="tpu_custom_call" | custom-call | tf_op jit(solution)/shard_map/pallas_call | solution.py:174
  2.9 7.7 %all-to-all-start = ((bf16[8,2,8,2,16,128]{5,4,3,2,1,0:T(8,128)(2,1)}), bf16[8,2,8,2,16,128]{5,4,3,2,1,0:T(8,128)(2,1)S(1)}, u32[]{:S(2)}, u32[]{:S(2)}) async-start(bf16[8,2,8,2,16,128]{5,4,3,2,1,0:T(8,128)(2,1)} %shard_map.77), calls=%async_computation | async-start | bytes 2097152 | tf_op jit(solution)/shard_map/all_to_all | solution.py:186
  10.6 0.0 copy-done
  10.6 4.0 %collective-permute-start = (bf16[8,4,128,128]{3,2,1,0:T(8,128)(2,1)S(1)}, bf16[8,4,128,128]{3,2,1,0:T(8,128)(2,1)}, u32[]{:S(2)}, u32[]{:S(2)}) collective-permute-start(bf16[8,4,128,128]{3,2,1,0:T(8,128)(2,1)S(1)} %copy-done), channel_id=1, source_target_pairs={{0,8},{8,16},{16,24},{24,32},{32,40},{40,48},{48,56},{56,64},{64,7... | collective-permute-start | bytes 3145736 | tf_op jit(solution)/shard_map/ppermute | solution.py:171
  14.6 13.1 %collective-permute-start.1 = (bf16[8,4,128,128]{3,2,1,0:T(8,128)(2,1)S(1)}, bf16[8,4,128,128]{3,2,1,0:T(8,128)(2,1)S(1)}, u32[]{:S(2)}, u32[]{:S(2)}) collective-permute-start(bf16[8,4,128,128]{3,2,1,0:T(8,128)(2,1)S(1)} %copy-done), channel_id=1, source_target_pairs={{8,0},{16,8},{24,16},{32,24},{40,32},{48,40},{56,48},{64,56},{72,6... | collective-permute-start | bytes 3145736 | tf_op jit(solution)/shard_map/ppermute | solution.py:172
  27.7 0.1 pad_add_fusion.spot_ref
  27.8 20.7 %collective-permute-done.low_ref = bf16[8,4,128,128]{3,2,1,0:T(8,128)(2,1)} collective-permute-done((bf16[8,4,128,128]{3,2,1,0:T(8,128)(2,1)S(1)}, bf16[8,4,128,128]{3,2,1,0:T(8,128)(2,1)}, u32[]{:S(2)}, u32[]{:S(2)}) %collective-permute-start) | collective-permute-done | bytes 1048608 | tf_op jit(solution)/shard_map/ppermute | solution.py:171
  48.4 0.0 all-to-all-done.tiles_ref
  48.4 0.0 copy-done.3
  48.4 0.0 copy-done.1
  48.4 0.0 copy-done.2
  48.4 2.4 %shard_map.78 = (f32[256,512]{1,0:T(8,128)S(1)}, bf16[256,3200]{1,0:T(8,128)(2,1)S(1)}) custom-call(s32[2]{0:T(128)S(1)} %pad_add_fusion.spot_ref, s32[8,16]{1,0:T(8,128)S(1)} %copy-done.1, s32[8]{0:T(128)S(1)} %copy-done.3, bf16[8,2,8,2,16,128]{5,4,3,2,1,0:T(8,128)(2,1)S(1)} %all-to-all-done.tiles_ref, ...), custom_call_target="tpu_custom_call" | custom-call | tf_op jit(solution)/shard_map/pallas_call | solution.py:190
  50.9 0.0 collective-permute-done.1.high_ref
  50.9 1.1 %shard_map.79 = (f32[8,4,16,128]{3,2,1,0:T(8,128)S(1)}, f32[8,4,16,128]{3,2,1,0:T(8,128)S(1)}, f32[64,1,128]{2,1,0:T(1,128)S(1)}) custom-call(f32[256,512]{1,0:T(8,128)S(1)} %get-tuple-element.7.total_ref, bf16[256,3200]{1,0:T(8,128)(2,1)S(1)} %get-tuple-element.8.oper_ref, bf16[8,4,128,128]{3,2,1,0:T(8,128)(2,1)S(1)} %collective-permute-done.1.high_ref), custom_call_target="tpu_custom_call" | custom-call | tf_op jit(solution)/shard_map/pallas_call | solution.py:204
  52.0 19.1 %all_to_all.15.parts_ref = f32[64,1,128]{2,1,0:T(1,128)S(1)} all-to-all(f32[64,1,128]{2,1,0:T(1,128)S(1)} %get-tuple-element.9), channel_id=1, replica_groups=mesh['row'=8,'col'=12,'state'=8] {'row','state'}, dimensions={0} | all-to-all | bytes 65536 | tf_op jit(solution)/shard_map/all_to_all | solution.py:212
  71.1 0.2 shard_map.80
  71.3 15.0 %all_to_all.16.parts_ref = f32[12,1,128]{2,1,0:T(1,128)S(1)} all-to-all(f32[12,1,128]{2,1,0:T(1,128)S(1)} %shard_map.80), channel_id=1, replica_groups=mesh['row'=8,'col'=12,'state'=8] {'col'}, dimensions={0} | all-to-all | bytes 12288 | tf_op jit(solution)/shard_map/all_to_all | solution.py:220
  86.3 0.9 %shard_map.81 = (f32[8,4,16,128]{3,2,1,0:T(8,128)}, f32[4]{0:T(128)}) custom-call(f32[12,1,128]{2,1,0:T(1,128)S(1)} %all_to_all.16.parts_ref, f32[8,4,16,128]{3,2,1,0:T(8,128)S(1)} %get-tuple-element.10.kx_ref, f32[8,4,16,128]{3,2,1,0:T(8,128)S(1)} %get-tuple-element.11.sx_ref), custom_call_target="tpu_custom_call" | custom-call | tf_op jit(solution)/shard_map/pallas_call | solution.py:221
Async XLA Ops:
  0.6 10.0 %copy-start = (bf16[8,4,128,128]{3,2,1,0:T(8,128)(2,1)S(1)}, bf16[8,4,128,128]{3,2,1,0:T(8,128)(2,1)}, u32[]{:S(2)}) copy-start(bf16[8,4,128,128]{3,2,1,0:T(8,128)(2,1)} %mid_ref.1) | copy-start | bytes 3145732
  0.6 47.8 %copy-start.3 = (s32[8]{0:T(128)S(1)}, s32[8]{0:T(128)}, u32[]{:S(2)}) copy-start(s32[8]{0:T(128)} %counts_ref.1) | copy-start | bytes 100
  0.7 47.8 %copy-start.1 = (s32[8,16]{1,0:T(8,128)S(1)}, s32[8,16]{1,0:T(8,128)}, u32[]{:S(2)}) copy-start(s32[8,16]{1,0:T(8,128)} %columns_ref.1) | copy-start | bytes 1540
  0.7 47.8 %copy-start.2 = (f32[8,16]{1,0:T(8,128)S(1)}, f32[8,16]{1,0:T(8,128)}, u32[]{:S(2)}) copy-start(f32[8,16]{1,0:T(8,128)} %onsite_ref.1) | copy-start | bytes 1540
  2.9 45.5 %all-to-all-start = ((bf16[8,2,8,2,16,128]{5,4,3,2,1,0:T(8,128)(2,1)}), bf16[8,2,8,2,16,128]{5,4,3,2,1,0:T(8,128)(2,1)S(1)}, u32[]{:S(2)}, u32[]{:S(2)}) async-start(bf16[8,2,8,2,16,128]{5,4,3,2,1,0:T(8,128)(2,1)} %shard_map.77), calls=%async_computation | async-start | bytes 2097152 | tf_op jit(solution)/shard_map/all_to_all | solution.py:186
  10.6 37.8 %collective-permute-start = (bf16[8,4,128,128]{3,2,1,0:T(8,128)(2,1)S(1)}, bf16[8,4,128,128]{3,2,1,0:T(8,128)(2,1)}, u32[]{:S(2)}, u32[]{:S(2)}) collective-permute-start(bf16[8,4,128,128]{3,2,1,0:T(8,128)(2,1)S(1)} %copy-done), channel_id=1, source_target_pairs={{0,8},{8,16},{16,24},{24,32},{32,40},{40,48},{48,56},{56,64},{64,7... | collective-permute-start | bytes 3145736 | tf_op jit(solution)/shard_map/ppermute | solution.py:171
  14.6 36.3 %collective-permute-start.1 = (bf16[8,4,128,128]{3,2,1,0:T(8,128)(2,1)S(1)}, bf16[8,4,128,128]{3,2,1,0:T(8,128)(2,1)S(1)}, u32[]{:S(2)}, u32[]{:S(2)}) collective-permute-start(bf16[8,4,128,128]{3,2,1,0:T(8,128)(2,1)S(1)} %copy-done), channel_id=1, source_target_pairs={{8,0},{16,8},{24,16},{32,24},{40,32},{48,40},{56,48},{64,56},{72,6... | collective-permute-start | bytes 3145736 | tf_op jit(solution)/shard_map/ppermute | solution.py:172

commit v3 on v2

--- a/solution.py
+++ b/solution.py
@@ -27,12 +27,13 @@
     return row
 
 
-def send_kernel(k_ref, s_ref, out_ref, held_ref, in_sems, out_sems):
+def send_kernel(lead, k_ref, s_ref, out_ref, held_ref, in_sems, out_sems):
     layers, _, _, _, own, _ = out_ref.shape
     pairs = [(d, op) for d in range(layers) for op in range(2)]
     loads = []
     for d, op in pairs:
-        part = (k_ref, s_ref)[op].at[:, :, pl.ds(d * own, own), :]
+        top = (lead + d) % layers * own
+        part = (k_ref, s_ref)[op].at[:, :, pl.ds(top, own), :]
         loads.append(pltpu.make_async_copy(part, held_ref.at[d, op], in_sems.at[d, op]))
         loads[-1].start()
     stores = []
@@ -72,7 +73,7 @@
 
 
 def early_kernel(
-    states, spot_ref, columns_ref, counts_ref, tiles_ref, low_ref, mid_ref, onsite_ref, total_ref, oper_ref
+    states, lead, spot_ref, columns_ref, counts_ref, tiles_ref, low_ref, mid_ref, onsite_ref, total_ref, oper_ref
 ):
     layers, _, rows, slot_dev, own, width = tiles_ref.shape
     half = rows * own
@@ -81,7 +82,7 @@
     for i in range(rows):
         for y in range(layers):
             for m in range(slot_dev):
-                slot = y * slot_dev + m
+                slot = (lead + y) % layers * slot_dev + m
                 block = columns_ref[i, slot] - spot_ref[0]
                 block = jnp.where(slot < counts_ref[i], block, window)
                 block = jnp.clip(block, 0, window)
@@ -156,6 +157,10 @@
         ritz_ref[s] = ritz[0, s]
 
 
+def ring_from(lead, size):
+    return [[(lead + k) % size for k in range(size)]]
+
+
 def per_device(vectors, onsite, k_tiles, s_tiles, columns, counts):
     rows_blk, states, width, _ = vectors.shape
     layers = lax.axis_size("state")
@@ -171,8 +176,9 @@
     low = lax.ppermute(vectors[rows_blk - REACH :], ("row", "col"), forward)
     high = lax.ppermute(vectors[:REACH], ("row", "col"), backward)
 
+    lead = layers // 2
     send = pl.pallas_call(
-        send_kernel,
+        functools.partial(send_kernel, lead),
         out_shape=jax.ShapeDtypeStruct((layers, 2, rows_blk, slot_dev, own, width), k_tiles.dtype),
         in_specs=[ANY, ANY],
         out_specs=ANY,
@@ -183,12 +189,14 @@
         ],
         compiler_params=limit(8),
     )(*(pltpu.with_memory_space_constraint(t, pltpu.HBM) for t in (k_tiles, s_tiles)))
-    tiles = lax.all_to_all(send, "state", 0, 0, tiled=True)
+    tiles = lax.all_to_all(
+        send, "state", 0, 0, axis_index_groups=ring_from(lead, layers), tiled=True
+    )
 
     spot = jnp.stack([device * rows_blk - REACH, layer])
     tall = 2 * rows_blk * own
     total, oper = pl.pallas_call(
-        functools.partial(early_kernel, states),
+        functools.partial(early_kernel, states, lead),
         out_shape=(
             jax.ShapeDtypeStruct((tall, states * width), jnp.float32),
             jax.ShapeDtypeStruct((tall, (window + 1) * width), vectors.dtype),
@@ -200,6 +208,8 @@
 
     inner = lax.axis_size(("row", "state"))
     outer = lax.axis_size("col")
+    late_plane = inner - 2 * layers + lead
+    late_col = outer // 2 + 1
     outs = jax.ShapeDtypeStruct((rows_blk, states, own, width), jnp.float32)
     kx, sx, stat = pl.pallas_call(
         functools.partial(late_kernel, states),
@@ -209,7 +219,9 @@
         compiler_params=limit(12),
     )(total, oper, high)
 
-    stat = lax.all_to_all(stat, ("row", "state"), 0, 0, tiled=True)
+    stat = lax.all_to_all(
+        stat, ("row", "state"), 0, 0, axis_index_groups=ring_from(late_plane, inner), tiled=True
+    )
     stat = pl.pallas_call(
         functools.partial(merge_kernel, states),
         out_shape=jax.ShapeDtypeStruct((outer, 1, width), jnp.float32),
@@ -217,7 +229,9 @@
         out_specs=VMEM,
         compiler_params=limit(2),
     )(stat)
-    stat = lax.all_to_all(stat, "col", 0, 0, tiled=True)
+    stat = lax.all_to_all(
+        stat, "col", 0, 0, axis_index_groups=ring_from(late_col, outer), tiled=True
+    )
     correction, ritz = pl.pallas_call(
         functools.partial(final_kernel, states, count * rows_blk * width * width),
         out_shape=(outs, jax.ShapeDtypeStruct((states,), jnp.float32)),

time: 87.5 us -> 81.2 us (0.928)
  blocking collectives: 34 us -> 25 us
  starting transfers between devices: 24.7 us -> 26.9 us
    all_to_all x2, blocking collectives: 34 us -> 25 us  [the longest x1 13.2 us: per_device(): lax.all_to_all(stat, ('row', 'state'), 0, 0, axis_index_groups=ring_from(...]
    all_to_all x1, starting transfers between devices: 7.66 us -> 9.86 us  [per_device(): lax.all_to_all(send, 'state', 0, 0, axis_index_groups=ring_from(lead, lay...]
where the time goes in v3:
time: 81.2 us; the launch traced here: 80.3 us
  starting transfers between devices  26.9 us (33%)
  blocking collectives  25 us (31%)
  waiting for transfers between devices  20.7 us (25%)
  Pallas kernels  6.91 us (9%)
    ppermute x1, waiting for transfers between devices, per_device(): low = lax.ppermute(vectors[rows_blk - REACH:], ('row', 'col'), forward)  20.7 us
    all_to_all x1, blocking collectives, per_device(): lax.all_to_all(stat, ('row', 'state'), 0, 0, axis_index_groups=ring_from(...  13.2 us
    ppermute x1, starting transfers between devices, per_device(): high = lax.ppermute(vectors[:REACH], ('row', 'col'), backward)  13.1 us
    all_to_all x1, blocking collectives, per_device(): lax.all_to_all(stat, 'col', 0, 0, axis_index_groups=ring_from(late_col, o...  11.7 us
    all_to_all x1, starting transfers between devices, per_device(): lax.all_to_all(send, 'state', 0, 0, axis_index_groups=ring_from(lead, lay...  9.86 us
    ppermute x1, starting transfers between devices, per_device(): low = lax.ppermute(vectors[rows_blk - REACH:], ('row', 'col'), forward)  3.99 us
    pallas_call x1, Pallas kernels, per_device(): pl.pallas_call(functools.partial(early_kernel, states, lead), out_shape=(...  2.4 us
    pallas_call x1, Pallas kernels, per_device(): pl.pallas_call(functools.partial(send_kernel, lead), out_shape=jax.ShapeD...  2.24 us
  transfers between devices with their start and end apart: 3, of which 1 were waited for; matrix products, arithmetic and copies ran while one was open for 0% of the time, Pallas kernels for 3%

profile of v3, /device:TPU:1, one launch (start us, length us, event | category | flops | bytes accessed | tf_op | source)
XLA Modules:
  0.0 80.3 jit_solution(13755393039424126791)
XLA Ops:
  0.6 0.0 copy-start
  0.6 0.0 copy-start.3
  0.7 0.0 copy-start.1
  0.7 0.0 copy-start.2
  0.7 2.2 %shard_map.77 = bf16[8,2,8,2,16,128]{5,4,3,2,1,0:T(8,128)(2,1)} custom-call(bf16[8,2,128,128]{3,2,1,0:T(8,128)(2,1)} %k_ref.1, bf16[8,2,128,128]{3,2,1,0:T(8,128)(2,1)} %s_ref.1), custom_call_target="tpu_custom_call" | custom-call | tf_op jit(solution)/shard_map/pallas_call | solution.py:180
  2.9 9.9 %all-to-all-start = ((bf16[8,2,8,2,16,128]{5,4,3,2,1,0:T(8,128)(2,1)}), bf16[8,2,8,2,16,128]{5,4,3,2,1,0:T(8,128)(2,1)S(1)}, u32[]{:S(2)}, u32[]{:S(2)}) async-start(bf16[8,2,8,2,16,128]{5,4,3,2,1,0:T(8,128)(2,1)} %shard_map.77), calls=%async_computation | async-start | bytes 2097152 | tf_op jit(solution)/shard_map/all_to_all | solution.py:192
  12.8 0.0 copy-done
  12.8 4.0 %collective-permute-start = (bf16[8,4,128,128]{3,2,1,0:T(8,128)(2,1)S(1)}, bf16[8,4,128,128]{3,2,1,0:T(8,128)(2,1)}, u32[]{:S(2)}, u32[]{:S(2)}) collective-permute-start(bf16[8,4,128,128]{3,2,1,0:T(8,128)(2,1)S(1)} %copy-done), channel_id=1, source_target_pairs={{0,8},{8,16},{16,24},{24,32},{32,40},{40,48},{48,56},{56,64},{64,7... | collective-permute-start | bytes 3145736 | tf_op jit(solution)/shard_map/ppermute | solution.py:176
  16.8 13.1 %collective-permute-start.1 = (bf16[8,4,128,128]{3,2,1,0:T(8,128)(2,1)S(1)}, bf16[8,4,128,128]{3,2,1,0:T(8,128)(2,1)S(1)}, u32[]{:S(2)}, u32[]{:S(2)}) collective-permute-start(bf16[8,4,128,128]{3,2,1,0:T(8,128)(2,1)S(1)} %copy-done), channel_id=1, source_target_pairs={{8,0},{16,8},{24,16},{32,24},{40,32},{48,40},{56,48},{64,56},{72,6... | collective-permute-start | bytes 3145736 | tf_op jit(solution)/shard_map/ppermute | solution.py:177
  29.9 0.1 pad_add_fusion.spot_ref
  30.0 20.7 %collective-permute-done.low_ref = bf16[8,4,128,128]{3,2,1,0:T(8,128)(2,1)} collective-permute-done((bf16[8,4,128,128]{3,2,1,0:T(8,128)(2,1)S(1)}, bf16[8,4,128,128]{3,2,1,0:T(8,128)(2,1)}, u32[]{:S(2)}, u32[]{:S(2)}) %collective-permute-start) | collective-permute-done | bytes 1048608 | tf_op jit(solution)/shard_map/ppermute | solution.py:176
  50.6 0.0 all-to-all-done.tiles_ref
  50.6 0.0 copy-done.3
  50.6 0.0 copy-done.1
  50.6 0.0 copy-done.2
  50.6 2.4 %shard_map.78 = (f32[256,512]{1,0:T(8,128)S(1)}, bf16[256,3200]{1,0:T(8,128)(2,1)S(1)}) custom-call(s32[2]{0:T(128)S(1)} %pad_add_fusion.spot_ref, s32[8,16]{1,0:T(8,128)S(1)} %copy-done.1, s32[8]{0:T(128)S(1)} %copy-done.3, bf16[8,2,8,2,16,128]{5,4,3,2,1,0:T(8,128)(2,1)S(1)} %all-to-all-done.tiles_ref, ...), custom_call_target="tpu_custom_call" | custom-call | tf_op jit(solution)/shard_map/pallas_call | solution.py:198
  53.0 0.0 collective-permute-done.1.high_ref
  53.0 1.1 %shard_map.79 = (f32[8,4,16,128]{3,2,1,0:T(8,128)S(1)}, f32[8,4,16,128]{3,2,1,0:T(8,128)S(1)}, f32[64,1,128]{2,1,0:T(1,128)S(1)}) custom-call(f32[256,512]{1,0:T(8,128)S(1)} %get-tuple-element.7.total_ref, bf16[256,3200]{1,0:T(8,128)(2,1)S(1)} %get-tuple-element.8.oper_ref, bf16[8,4,128,128]{3,2,1,0:T(8,128)(2,1)S(1)} %collective-permute-done.1.high_ref), custom_call_target="tpu_custom_call" | custom-call | tf_op jit(solution)/shard_map/pallas_call | solution.py:214
  54.2 13.2 %all_to_all.15.parts_ref = f32[64,1,128]{2,1,0:T(1,128)S(1)} all-to-all(f32[64,1,128]{2,1,0:T(1,128)S(1)} %get-tuple-element.9), channel_id=1, replica_groups={{580,581,582,583,672,673,674,675,676,677,678,679,0,1,2,3,4,5,6,7,96,97,..., dimensions={0} | all-to-all | bytes 65536 | tf_op jit(solution)/shard_map/all_to_all | solution.py:222
  67.5 0.2 shard_map.80
  67.6 11.7 %all_to_all.16.parts_ref = f32[12,1,128]{2,1,0:T(1,128)S(1)} all-to-all(f32[12,1,128]{2,1,0:T(1,128)S(1)} %shard_map.80), channel_id=1, replica_groups={{56,64,72,80,88,0,8,16,24,32,40,48},{57,65,73,81,89,1,9,17,25,33,41,49}..., dimensions={0} | all-to-all | bytes 12288 | tf_op jit(solution)/shard_map/all_to_all | solution.py:232
  79.4 0.9 %shard_map.81 = (f32[8,4,16,128]{3,2,1,0:T(8,128)}, f32[4]{0:T(128)}) custom-call(f32[12,1,128]{2,1,0:T(1,128)S(1)} %all_to_all.16.parts_ref, f32[8,4,16,128]{3,2,1,0:T(8,128)S(1)} %get-tuple-element.10.kx_ref, f32[8,4,16,128]{3,2,1,0:T(8,128)S(1)} %get-tuple-element.11.sx_ref), custom_call_target="tpu_custom_call" | custom-call | tf_op jit(solution)/shard_map/pallas_call | solution.py:235
Async XLA Ops:
  0.6 12.2 %copy-start = (bf16[8,4,128,128]{3,2,1,0:T(8,128)(2,1)S(1)}, bf16[8,4,128,128]{3,2,1,0:T(8,128)(2,1)}, u32[]{:S(2)}) copy-start(bf16[8,4,128,128]{3,2,1,0:T(8,128)(2,1)} %mid_ref.1) | copy-start | bytes 3145732
  0.6 50.0 %copy-start.3 = (s32[8]{0:T(128)S(1)}, s32[8]{0:T(128)}, u32[]{:S(2)}) copy-start(s32[8]{0:T(128)} %counts_ref.1) | copy-start | bytes 100
  0.7 50.0 %copy-start.1 = (s32[8,16]{1,0:T(8,128)S(1)}, s32[8,16]{1,0:T(8,128)}, u32[]{:S(2)}) copy-start(s32[8,16]{1,0:T(8,128)} %columns_ref.1) | copy-start | bytes 1540
  0.7 50.0 %copy-start.2 = (f32[8,16]{1,0:T(8,128)S(1)}, f32[8,16]{1,0:T(8,128)}, u32[]{:S(2)}) copy-start(f32[8,16]{1,0:T(8,128)} %onsite_ref.1) | copy-start | bytes 1540
  2.9 47.7 %all-to-all-start = ((bf16[8,2,8,2,16,128]{5,4,3,2,1,0:T(8,128)(2,1)}), bf16[8,2,8,2,16,128]{5,4,3,2,1,0:T(8,128)(2,1)S(1)}, u32[]{:S(2)}, u32[]{:S(2)}) async-start(bf16[8,2,8,2,16,128]{5,4,3,2,1,0:T(8,128)(2,1)} %shard_map.77), calls=%async_computation | async-start | bytes 2097152 | tf_op jit(solution)/shard_map/all_to_all | solution.py:192
  12.8 37.8 %collective-permute-start = (bf16[8,4,128,128]{3,2,1,0:T(8,128)(2,1)S(1)}, bf16[8,4,128,128]{3,2,1,0:T(8,128)(2,1)}, u32[]{:S(2)}, u32[]{:S(2)}) collective-permute-start(bf16[8,4,128,128]{3,2,1,0:T(8,128)(2,1)S(1)} %copy-done), channel_id=1, source_target_pairs={{0,8},{8,16},{16,24},{24,32},{32,40},{40,48},{48,56},{56,64},{64,7... | collective-permute-start | bytes 3145736 | tf_op jit(solution)/shard_map/ppermute | solution.py:176
  16.8 36.3 %collective-permute-start.1 = (bf16[8,4,128,128]{3,2,1,0:T(8,128)(2,1)S(1)}, bf16[8,4,128,128]{3,2,1,0:T(8,128)(2,1)S(1)}, u32[]{:S(2)}, u32[]{:S(2)}) collective-permute-start(bf16[8,4,128,128]{3,2,1,0:T(8,128)(2,1)S(1)} %copy-done), channel_id=1, source_target_pairs={{8,0},{16,8},{24,16},{32,24},{40,32},{48,40},{56,48},{64,56},{72,6... | collective-permute-start | bytes 3145736 | tf_op jit(solution)/shard_map/ppermute | solution.py:177

commit v4 on v2

--- a/solution.py
+++ b/solution.py
@@ -27,12 +27,13 @@
     return row
 
 
-def send_kernel(k_ref, s_ref, out_ref, held_ref, in_sems, out_sems):
+def send_kernel(order, k_ref, s_ref, out_ref, held_ref, in_sems, out_sems):
     layers, _, _, _, own, _ = out_ref.shape
     pairs = [(d, op) for d in range(layers) for op in range(2)]
     loads = []
     for d, op in pairs:
-        part = (k_ref, s_ref)[op].at[:, :, pl.ds(d * own, own), :]
+        top = order[d] * own
+        part = (k_ref, s_ref)[op].at[:, :, pl.ds(top, own), :]
         loads.append(pltpu.make_async_copy(part, held_ref.at[d, op], in_sems.at[d, op]))
         loads[-1].start()
     stores = []
@@ -72,7 +73,7 @@
 
 
 def early_kernel(
-    states, spot_ref, columns_ref, counts_ref, tiles_ref, low_ref, mid_ref, onsite_ref, total_ref, oper_ref
+    states, order, spot_ref, columns_ref, counts_ref, tiles_ref, low_ref, mid_ref, onsite_ref, total_ref, oper_ref
 ):
     layers, _, rows, slot_dev, own, width = tiles_ref.shape
     half = rows * own
@@ -81,7 +82,7 @@
     for i in range(rows):
         for y in range(layers):
             for m in range(slot_dev):
-                slot = y * slot_dev + m
+                slot = order[y] * slot_dev + m
                 block = columns_ref[i, slot] - spot_ref[0]
                 block = jnp.where(slot < counts_ref[i], block, window)
                 block = jnp.clip(block, 0, window)
@@ -133,13 +134,19 @@
             sx = total[half:, t * width : (t + 1) * width]
             kx_ref[:, s + t] = kx.reshape(rows, own, width)
             sx_ref[:, s + t] = sx.reshape(rows, own, width)
-            p = jnp.sum(sx * sx, keepdims=True)
-            c = jnp.sum(sx * kx, keepdims=True)
-            resid = kx - (c / (p + EPS)) * sx
-            power.append(p)
-            cross.append(c)
-            norm.append(jnp.sum(resid * resid, keepdims=True))
-    row = lanes(power + cross + norm)
+            power.append(jnp.sum(sx * sx, axis=0, keepdims=True))
+            cross.append(jnp.sum(sx * kx, axis=0, keepdims=True))
+    sums = jnp.sum(jnp.concatenate(power + cross, axis=0), axis=1, keepdims=True)
+    ratio = sums[states:] / (sums[:states] + EPS)
+    for s in range(states):
+        resid = kx_ref[:, s] - ratio[s : s + 1][None] * sx_ref[:, s]
+        resid = resid.reshape(half, width)
+        norm.append(jnp.sum(resid * resid, axis=0, keepdims=True))
+    norm = jnp.sum(jnp.concatenate(norm, axis=0), axis=1, keepdims=True)
+    column = jnp.concatenate([sums, norm], axis=0)
+    shape = (3 * states, width)
+    mine = lax.broadcasted_iota(jnp.int32, shape, 0) == lax.broadcasted_iota(jnp.int32, shape, 1)
+    row = jnp.sum(jnp.where(mine, jnp.broadcast_to(column, shape), 0.0), axis=0, keepdims=True)
     stat_ref[...] = jnp.broadcast_to(row[None], stat_ref.shape)
 
 
@@ -154,6 +161,25 @@
     for s in range(states):
         out_ref[:, s] = (kx_ref[:, s] - pick(ritz, s)[None] * sx_ref[:, s]) * pick(scale, s)[None]
         ritz_ref[s] = ritz[0, s]
+
+
+def led(group, lead):
+    return [lead] + [m for m in group if m != lead]
+
+
+def sum_phases(rows, cols, layers):
+    lines = [
+        led([row * cols + c for row in (x, x + 1) for c in range(cols)], x * cols + cols // 2 + 1)
+        for x in range(0, rows, 2)
+    ]
+    planes = [
+        led(
+            [row * layers + m for row in range(core, rows, 2) for m in range(layers)],
+            (rows - 2 + core) * layers + layers // 2,
+        )
+        for core in range(2)
+    ]
+    return [(("row", "col"), lines), (("row", "state"), planes)]
 
 
 def per_device(vectors, onsite, k_tiles, s_tiles, columns, counts):
@@ -171,8 +197,10 @@
     low = lax.ppermute(vectors[rows_blk - REACH :], ("row", "col"), forward)
     high = lax.ppermute(vectors[:REACH], ("row", "col"), backward)
 
+    half = layers // 2
+    order = [k // 2 + (half if k % 2 == 0 else 0) for k in range(layers)]
     send = pl.pallas_call(
-        send_kernel,
+        functools.partial(send_kernel, order),
         out_shape=jax.ShapeDtypeStruct((layers, 2, rows_blk, slot_dev, own, width), k_tiles.dtype),
         in_specs=[ANY, ANY],
         out_specs=ANY,
@@ -183,12 +211,14 @@
         ],
         compiler_params=limit(8),
     )(*(pltpu.with_memory_space_constraint(t, pltpu.HBM) for t in (k_tiles, s_tiles)))
-    tiles = lax.all_to_all(send, "state", 0, 0, tiled=True)
+    tiles = lax.all_to_all(
+        send, "state", 0, 0, axis_index_groups=[order], tiled=True
+    )
 
     spot = jnp.stack([device * rows_blk - REACH, layer])
     tall = 2 * rows_blk * own
     total, oper = pl.pallas_call(
-        functools.partial(early_kernel, states),
+        functools.partial(early_kernel, states, order),
         out_shape=(
             jax.ShapeDtypeStruct((tall, states * width), jnp.float32),
             jax.ShapeDtypeStruct((tall, (window + 1) * width), vectors.dtype),
@@ -198,8 +228,8 @@
         compiler_params=limit(12),
     )(spot, columns, counts, tiles, low, vectors, onsite)
 
-    inner = lax.axis_size(("row", "state"))
-    outer = lax.axis_size("col")
+    phases = sum_phases(lax.axis_size("row"), lax.axis_size("col"), layers)
+    inner, outer = (len(groups[0]) for _, groups in phases)
     outs = jax.ShapeDtypeStruct((rows_blk, states, own, width), jnp.float32)
     kx, sx, stat = pl.pallas_call(
         functools.partial(late_kernel, states),
@@ -209,7 +239,8 @@
         compiler_params=limit(12),
     )(total, oper, high)
 
-    stat = lax.all_to_all(stat, ("row", "state"), 0, 0, tiled=True)
+    axes, groups = phases[0]
+    stat = lax.all_to_all(stat, axes, 0, 0, axis_index_groups=groups, tiled=True)
     stat = pl.pallas_call(
         functools.partial(merge_kernel, states),
         out_shape=jax.ShapeDtypeStruct((outer, 1, width), jnp.float32),
@@ -217,7 +248,8 @@
         out_specs=VMEM,
         compiler_params=limit(2),
     )(stat)
-    stat = lax.all_to_all(stat, "col", 0, 0, tiled=True)
+    axes, groups = phases[1]
+    stat = lax.all_to_all(stat, axes, 0, 0, axis_index_groups=groups, tiled=True)
     correction, ritz = pl.pallas_call(
         functools.partial(final_kernel, states, count * rows_blk * width * width),
         out_shape=(outs, jax.ShapeDtypeStruct((states,), jnp.float32)),

time: 87.5 us -> 80.4 us (0.919)
  blocking collectives: 34 us -> 24.6 us
  starting transfers between devices: 24.7 us -> 26.9 us
    all_to_all x2, blocking collectives: 34 us -> 24.6 us  [per_device(): lax.all_to_all(stat, axes, 0, 0, axis_index_groups=groups, tiled=True)]
    all_to_all x1, starting transfers between devices: 7.66 us -> 9.84 us  [per_device(): lax.all_to_all(send, 'state', 0, 0, axis_index_groups=[order], tiled=True)]
where the time goes in v4:
time: 80.4 us; the launch traced here: 79.6 us
  starting transfers between devices  26.9 us (33%)
  blocking collectives  24.6 us (31%)
  waiting for transfers between devices  20.7 us (26%)
  Pallas kernels  6.56 us (8%)
    all_to_all x2, blocking collectives, per_device(): lax.all_to_all(stat, axes, 0, 0, axis_index_groups=groups, tiled=True)  24.6 us
    ppermute x1, waiting for transfers between devices, per_device(): low = lax.ppermute(vectors[rows_blk - REACH:], ('row', 'col'), forward)  20.7 us
    ppermute x1, starting transfers between devices, per_device(): high = lax.ppermute(vectors[:REACH], ('row', 'col'), backward)  13.1 us
    all_to_all x1, starting transfers between devices, per_device(): lax.all_to_all(send, 'state', 0, 0, axis_index_groups=[order], tiled=True)  9.84 us
    ppermute x1, starting transfers between devices, per_device(): low = lax.ppermute(vectors[rows_blk - REACH:], ('row', 'col'), forward)  3.99 us
    pallas_call x1, Pallas kernels, per_device(): pl.pallas_call(functools.partial(early_kernel, states, order), out_shape=...  2.4 us
    pallas_call x1, Pallas kernels, per_device(): pl.pallas_call(functools.partial(send_kernel, order), out_shape=jax.Shape...  2.24 us
  transfers between devices with their start and end apart: 3, of which 1 were waited for; matrix products, arithmetic and copies ran while one was open for 0% of the time, Pallas kernels for 3%

profile of v4, /device:TPU:1, one launch (start us, length us, event | category | flops | bytes accessed | tf_op | source)
XLA Modules:
  0.0 79.6 jit_solution(8478156145106819486)
XLA Ops:
  0.6 0.0 copy-start
  0.6 0.0 copy-start.3
  0.7 0.0 copy-start.1
  0.7 0.0 copy-start.2
  0.7 2.2 %shard_map.77 = bf16[8,2,8,2,16,128]{5,4,3,2,1,0:T(8,128)(2,1)} custom-call(bf16[8,2,128,128]{3,2,1,0:T(8,128)(2,1)} %k_ref.1, bf16[8,2,128,128]{3,2,1,0:T(8,128)(2,1)} %s_ref.1), custom_call_target="tpu_custom_call" | custom-call | tf_op jit(solution)/shard_map/pallas_call | solution.py:202
  2.9 9.8 %all-to-all-start = ((bf16[8,2,8,2,16,128]{5,4,3,2,1,0:T(8,128)(2,1)}), bf16[8,2,8,2,16,128]{5,4,3,2,1,0:T(8,128)(2,1)S(1)}, u32[]{:S(2)}, u32[]{:S(2)}) async-start(bf16[8,2,8,2,16,128]{5,4,3,2,1,0:T(8,128)(2,1)} %shard_map.77), calls=%async_computation | async-start | bytes 2097152 | tf_op jit(solution)/shard_map/all_to_all | solution.py:214
  12.8 0.0 copy-done
  12.8 4.0 %collective-permute-start = (bf16[8,4,128,128]{3,2,1,0:T(8,128)(2,1)S(1)}, bf16[8,4,128,128]{3,2,1,0:T(8,128)(2,1)}, u32[]{:S(2)}, u32[]{:S(2)}) collective-permute-start(bf16[8,4,128,128]{3,2,1,0:T(8,128)(2,1)S(1)} %copy-done), channel_id=1, source_target_pairs={{0,8},{8,16},{16,24},{24,32},{32,40},{40,48},{48,56},{56,64},{64,7... | collective-permute-start | bytes 3145736 | tf_op jit(solution)/shard_map/ppermute | solution.py:197
  16.8 13.1 %collective-permute-start.1 = (bf16[8,4,128,128]{3,2,1,0:T(8,128)(2,1)S(1)}, bf16[8,4,128,128]{3,2,1,0:T(8,128)(2,1)S(1)}, u32[]{:S(2)}, u32[]{:S(2)}) collective-permute-start(bf16[8,4,128,128]{3,2,1,0:T(8,128)(2,1)S(1)} %copy-done), channel_id=1, source_target_pairs={{8,0},{16,8},{24,16},{32,24},{40,32},{48,40},{56,48},{64,56},{72,6... | collective-permute-start | bytes 3145736 | tf_op jit(solution)/shard_map/ppermute | solution.py:198
  29.9 0.1 pad_add_fusion.spot_ref
  29.9 20.7 %collective-permute-done.low_ref = bf16[8,4,128,128]{3,2,1,0:T(8,128)(2,1)} collective-permute-done((bf16[8,4,128,128]{3,2,1,0:T(8,128)(2,1)S(1)}, bf16[8,4,128,128]{3,2,1,0:T(8,128)(2,1)}, u32[]{:S(2)}, u32[]{:S(2)}) %collective-permute-start) | collective-permute-done | bytes 1048608 | tf_op jit(solution)/shard_map/ppermute | solution.py:197
  50.6 0.0 all-to-all-done.tiles_ref
  50.6 0.0 copy-done.3
  50.6 0.0 copy-done.1
  50.6 0.0 copy-done.2
  50.6 2.4 %shard_map.78 = (f32[256,512]{1,0:T(8,128)S(1)}, bf16[256,3200]{1,0:T(8,128)(2,1)S(1)}) custom-call(s32[2]{0:T(128)S(1)} %pad_add_fusion.spot_ref, s32[8,16]{1,0:T(8,128)S(1)} %copy-done.1, s32[8]{0:T(128)S(1)} %copy-done.3, bf16[8,2,8,2,16,128]{5,4,3,2,1,0:T(8,128)(2,1)S(1)} %all-to-all-done.tiles_ref, ...), custom_call_target="tpu_custom_call" | custom-call | tf_op jit(solution)/shard_map/pallas_call | solution.py:220
  53.0 0.0 collective-permute-done.1.high_ref
  53.0 0.8 %shard_map.79 = (f32[8,4,16,128]{3,2,1,0:T(8,128)S(1)}, f32[8,4,16,128]{3,2,1,0:T(8,128)S(1)}, f32[24,1,128]{2,1,0:T(1,128)S(1)}) custom-call(f32[256,512]{1,0:T(8,128)S(1)} %get-tuple-element.7.total_ref, bf16[256,3200]{1,0:T(8,128)(2,1)S(1)} %get-tuple-element.8.oper_ref, bf16[8,4,128,128]{3,2,1,0:T(8,128)(2,1)S(1)} %collective-permute-done.1.high_ref), custom_call_target="tpu_custom_call" | custom-call | tf_op jit(solution)/shard_map/pallas_call | solution.py:234
  53.8 12.6 %all_to_all.15.parts_ref = f32[24,1,128]{2,1,0:T(1,128)S(1)} all-to-all(f32[24,1,128]{2,1,0:T(1,128)S(1)} %get-tuple-element.9), channel_id=1, replica_groups={{56,0,8,16,24,32,40,48,64,72,80,88,96,104,112,120,128,136,144,152,160,1..., dimensions={0} | all-to-all | bytes 24576 | tf_op jit(solution)/shard_map/all_to_all | solution.py:243
  66.5 0.2 shard_map.80
  66.7 12.0 %all_to_all.16.parts_ref = f32[32,1,128]{2,1,0:T(1,128)S(1)} all-to-all(f32[32,1,128]{2,1,0:T(1,128)S(1)} %shard_map.80), channel_id=1, replica_groups={{580,0,1,2,3,4,5,6,7,192,193,194,195,196,197,198,199,384,385,386,387,38..., dimensions={0} | all-to-all | bytes 32768 | tf_op jit(solution)/shard_map/all_to_all | solution.py:252
  78.7 0.9 %shard_map.81 = (f32[8,4,16,128]{3,2,1,0:T(8,128)}, f32[4]{0:T(128)}) custom-call(f32[32,1,128]{2,1,0:T(1,128)S(1)} %all_to_all.16.parts_ref, f32[8,4,16,128]{3,2,1,0:T(8,128)S(1)} %get-tuple-element.10.kx_ref, f32[8,4,16,128]{3,2,1,0:T(8,128)S(1)} %get-tuple-element.11.sx_ref), custom_call_target="tpu_custom_call" | custom-call | tf_op jit(solution)/shard_map/pallas_call | solution.py:253
Async XLA Ops:
  0.6 12.1 %copy-start = (bf16[8,4,128,128]{3,2,1,0:T(8,128)(2,1)S(1)}, bf16[8,4,128,128]{3,2,1,0:T(8,128)(2,1)}, u32[]{:S(2)}) copy-start(bf16[8,4,128,128]{3,2,1,0:T(8,128)(2,1)} %mid_ref.1) | copy-start | bytes 3145732
  0.6 50.0 %copy-start.3 = (s32[8]{0:T(128)S(1)}, s32[8]{0:T(128)}, u32[]{:S(2)}) copy-start(s32[8]{0:T(128)} %counts_ref.1) | copy-start | bytes 100
  0.7 49.9 %copy-start.1 = (s32[8,16]{1,0:T(8,128)S(1)}, s32[8,16]{1,0:T(8,128)}, u32[]{:S(2)}) copy-start(s32[8,16]{1,0:T(8,128)} %columns_ref.1) | copy-start | bytes 1540
  0.7 49.9 %copy-start.2 = (f32[8,16]{1,0:T(8,128)S(1)}, f32[8,16]{1,0:T(8,128)}, u32[]{:S(2)}) copy-start(f32[8,16]{1,0:T(8,128)} %onsite_ref.1) | copy-start | bytes 1540
  2.9 47.7 %all-to-all-start = ((bf16[8,2,8,2,16,128]{5,4,3,2,1,0:T(8,128)(2,1)}), bf16[8,2,8,2,16,128]{5,4,3,2,1,0:T(8,128)(2,1)S(1)}, u32[]{:S(2)}, u32[]{:S(2)}) async-start(bf16[8,2,8,2,16,128]{5,4,3,2,1,0:T(8,128)(2,1)} %shard_map.77), calls=%async_computation | async-start | bytes 2097152 | tf_op jit(solution)/shard_map/all_to_all | solution.py:214
  12.8 37.8 %collective-permute-start = (bf16[8,4,128,128]{3,2,1,0:T(8,128)(2,1)S(1)}, bf16[8,4,128,128]{3,2,1,0:T(8,128)(2,1)}, u32[]{:S(2)}, u32[]{:S(2)}) collective-permute-start(bf16[8,4,128,128]{3,2,1,0:T(8,128)(2,1)S(1)} %copy-done), channel_id=1, source_target_pairs={{0,8},{8,16},{16,24},{24,32},{32,40},{40,48},{48,56},{56,64},{64,7... | collective-permute-start | bytes 3145736 | tf_op jit(solution)/shard_map/ppermute | solution.py:197
  16.8 36.3 %collective-permute-start.1 = (bf16[8,4,128,128]{3,2,1,0:T(8,128)(2,1)S(1)}, bf16[8,4,128,128]{3,2,1,0:T(8,128)(2,1)S(1)}, u32[]{:S(2)}, u32[]{:S(2)}) collective-permute-start(bf16[8,4,128,128]{3,2,1,0:T(8,128)(2,1)S(1)} %copy-done), channel_id=1, source_target_pairs={{8,0},{16,8},{24,16},{32,24},{40,32},{48,40},{56,48},{64,56},{72,6... | collective-permute-start | bytes 3145736 | tf_op jit(solution)/shard_map/ppermute | solution.py:198

commit v5 on v4

--- a/solution.py
+++ b/solution.py
@@ -155,12 +155,23 @@
     stat_ref[...] = jnp.broadcast_to(packed(power, cross, norm, states)[None], stat_ref.shape)
 
 
-def final_kernel(states, cells, parts_ref, kx_ref, sx_ref, out_ref, ritz_ref):
+def final_kernel(states, cells, parts_ref, kx_ref, sx_ref, out_ref, ritz_ref, held_ref, sems):
     _, _, norm, ritz = merged_rows(parts_ref[...].reshape(parts_ref.shape[0], -1), states)
     scale = lax.rsqrt(norm / cells + EPS)
+    rows = held_ref.shape[0]
+    part = rows // 2
+    stores = []
+    for n in range(2):
+        here = pl.ds(n * part, part)
+        for s in range(states):
+            resid = kx_ref[here, s] - pick(ritz, s)[None] * sx_ref[here, s]
+            held_ref[here, s] = resid * pick(scale, s)[None]
+        stores.append(pltpu.make_async_copy(held_ref.at[here], out_ref.at[here], sems.at[n]))
+        stores[-1].start()
     for s in range(states):
-        out_ref[:, s] = (kx_ref[:, s] - pick(ritz, s)[None] * sx_ref[:, s]) * pick(scale, s)[None]
         ritz_ref[s] = ritz[0, s]
+    for store in stores:
+        store.wait()
 
 
 def led(group, lead):
@@ -169,7 +180,7 @@
 
 def sum_phases(rows, cols, layers):
     lines = [
-        led([row * cols + c for row in (x, x + 1) for c in range(cols)], x * cols + cols // 2 + 1)
+        led([row * cols + c for row in (x, x + 1) for c in range(cols)], (x + 1) * cols + cols // 2 + 1)
         for x in range(0, rows, 2)
     ]
     planes = [
@@ -254,7 +265,11 @@
         functools.partial(final_kernel, states, count * rows_blk * width * width),
         out_shape=(outs, jax.ShapeDtypeStruct((states,), jnp.float32)),
         in_specs=[VMEM] * 3,
-        out_specs=(VMEM, SMEM),
+        out_specs=(ANY, SMEM),
+        scratch_shapes=[
+            pltpu.VMEM((rows_blk, states, own, width), jnp.float32),
+            pltpu.SemaphoreType.DMA((2,)),
+        ],
         compiler_params=limit(4),
     )(stat, kx, sx)
     return correction, ritz

time: 80.4 us -> 80.7 us (level)
  no operation moved by 1% of the time
where the time goes in v5:
time: 80.7 us; the launch traced here: 79.8 us
  starting transfers between devices  26.9 us (33%)
  blocking collectives  24.3 us (30%)
  waiting for transfers between devices  20.7 us (26%)
  Pallas kernels  7.08 us (9%)
    all_to_all x2, blocking collectives, per_device(): lax.all_to_all(stat, axes, 0, 0, axis_index_groups=groups, tiled=True)  24.3 us
    ppermute x1, waiting for transfers between devices, per_device(): low = lax.ppermute(vectors[rows_blk - REACH:], ('row', 'col'), forward)  20.7 us
    ppermute x1, starting transfers between devices, per_device(): high = lax.ppermute(vectors[:REACH], ('row', 'col'), backward)  13.1 us
    all_to_all x1, starting transfers between devices, per_device(): lax.all_to_all(send, 'state', 0, 0, axis_index_groups=[order], tiled=True)  9.84 us
    ppermute x1, starting transfers between devices, per_device(): low = lax.ppermute(vectors[rows_blk - REACH:], ('row', 'col'), forward)  3.99 us
    pallas_call x1, Pallas kernels, per_device(): pl.pallas_call(functools.partial(early_kernel, states, order), out_shape=...  2.4 us
    pallas_call x1, Pallas kernels, per_device(): pl.pallas_call(functools.partial(send_kernel, order), out_shape=jax.Shape...  2.24 us
  transfers between devices with their start and end apart: 3, of which 1 were waited for; matrix products, arithmetic and copies ran while one was open for 0% of the time, Pallas kernels for 3%

profile of v5, /device:TPU:1, one launch (start us, length us, event | category | flops | bytes accessed | tf_op | source)
XLA Modules:
  0.0 79.8 jit_solution(270869310015115868)
XLA Ops:
  0.6 0.0 copy-start
  0.6 0.0 copy-start.3
  0.7 0.0 copy-start.1
  0.7 0.0 copy-start.2
  0.7 2.2 %shard_map.77 = bf16[8,2,8,2,16,128]{5,4,3,2,1,0:T(8,128)(2,1)} custom-call(bf16[8,2,128,128]{3,2,1,0:T(8,128)(2,1)} %k_ref.1, bf16[8,2,128,128]{3,2,1,0:T(8,128)(2,1)} %s_ref.1), custom_call_target="tpu_custom_call" | custom-call | tf_op jit(solution)/shard_map/pallas_call | solution.py:213
  2.9 9.8 %all-to-all-start = ((bf16[8,2,8,2,16,128]{5,4,3,2,1,0:T(8,128)(2,1)}), bf16[8,2,8,2,16,128]{5,4,3,2,1,0:T(8,128)(2,1)S(1)}, u32[]{:S(2)}, u32[]{:S(2)}) async-start(bf16[8,2,8,2,16,128]{5,4,3,2,1,0:T(8,128)(2,1)} %shard_map.77), calls=%async_computation | async-start | bytes 2097152 | tf_op jit(solution)/shard_map/all_to_all | solution.py:225
  12.8 0.0 copy-done
  12.8 4.0 %collective-permute-start = (bf16[8,4,128,128]{3,2,1,0:T(8,128)(2,1)S(1)}, bf16[8,4,128,128]{3,2,1,0:T(8,128)(2,1)}, u32[]{:S(2)}, u32[]{:S(2)}) collective-permute-start(bf16[8,4,128,128]{3,2,1,0:T(8,128)(2,1)S(1)} %copy-done), channel_id=1, source_target_pairs={{0,8},{8,16},{16,24},{24,32},{32,40},{40,48},{48,56},{56,64},{64,7... | collective-permute-start | bytes 3145736 | tf_op jit(solution)/shard_map/ppermute | solution.py:208
  16.8 13.1 %collective-permute-start.1 = (bf16[8,4,128,128]{3,2,1,0:T(8,128)(2,1)S(1)}, bf16[8,4,128,128]{3,2,1,0:T(8,128)(2,1)S(1)}, u32[]{:S(2)}, u32[]{:S(2)}) collective-permute-start(bf16[8,4,128,128]{3,2,1,0:T(8,128)(2,1)S(1)} %copy-done), channel_id=1, source_target_pairs={{8,0},{16,8},{24,16},{32,24},{40,32},{48,40},{56,48},{64,56},{72,6... | collective-permute-start | bytes 3145736 | tf_op jit(solution)/shard_map/ppermute | solution.py:209
  29.9 0.1 pad_add_fusion.spot_ref
  29.9 20.7 %collective-permute-done.low_ref = bf16[8,4,128,128]{3,2,1,0:T(8,128)(2,1)} collective-permute-done((bf16[8,4,128,128]{3,2,1,0:T(8,128)(2,1)S(1)}, bf16[8,4,128,128]{3,2,1,0:T(8,128)(2,1)}, u32[]{:S(2)}, u32[]{:S(2)}) %collective-permute-start) | collective-permute-done | bytes 1048608 | tf_op jit(solution)/shard_map/ppermute | solution.py:208
  50.6 0.0 all-to-all-done.tiles_ref
  50.6 0.0 copy-done.3
  50.6 0.0 copy-done.1
  50.6 0.0 copy-done.2
  50.6 2.4 %shard_map.78 = (f32[256,512]{1,0:T(8,128)S(1)}, bf16[256,3200]{1,0:T(8,128)(2,1)S(1)}) custom-call(s32[2]{0:T(128)S(1)} %pad_add_fusion.spot_ref, s32[8,16]{1,0:T(8,128)S(1)} %copy-done.1, s32[8]{0:T(128)S(1)} %copy-done.3, bf16[8,2,8,2,16,128]{5,4,3,2,1,0:T(8,128)(2,1)S(1)} %all-to-all-done.tiles_ref, ...), custom_call_target="tpu_custom_call" | custom-call | tf_op jit(solution)/shard_map/pallas_call | solution.py:231
  53.0 0.0 collective-permute-done.1.high_ref
  53.0 0.8 %shard_map.79 = (f32[8,4,16,128]{3,2,1,0:T(8,128)S(1)}, f32[8,4,16,128]{3,2,1,0:T(8,128)S(1)}, f32[24,1,128]{2,1,0:T(1,128)S(1)}) custom-call(f32[256,512]{1,0:T(8,128)S(1)} %get-tuple-element.7.total_ref, bf16[256,3200]{1,0:T(8,128)(2,1)S(1)} %get-tuple-element.8.oper_ref, bf16[8,4,128,128]{3,2,1,0:T(8,128)(2,1)S(1)} %collective-permute-done.1.high_ref), custom_call_target="tpu_custom_call" | custom-call | tf_op jit(solution)/shard_map/pallas_call | solution.py:245
  53.8 12.3 %all_to_all.15.parts_ref = f32[24,1,128]{2,1,0:T(1,128)S(1)} all-to-all(f32[24,1,128]{2,1,0:T(1,128)S(1)} %get-tuple-element.9), channel_id=1, replica_groups={{152,0,8,16,24,32,40,48,56,64,72,80,88,96,104,112,120,128,136,144,160,1..., dimensions={0} | all-to-all | bytes 24576 | tf_op jit(solution)/shard_map/all_to_all | solution.py:254
  66.1 0.2 shard_map.80
  66.3 12.0 %all_to_all.16.parts_ref = f32[32,1,128]{2,1,0:T(1,128)S(1)} all-to-all(f32[32,1,128]{2,1,0:T(1,128)S(1)} %shard_map.80), channel_id=1, replica_groups={{580,0,1,2,3,4,5,6,7,192,193,194,195,196,197,198,199,384,385,386,387,38..., dimensions={0} | all-to-all | bytes 32768 | tf_op jit(solution)/shard_map/all_to_all | solution.py:263
  78.3 1.4 %shard_map.81 = (f32[8,4,16,128]{3,2,1,0:T(8,128)}, f32[4]{0:T(128)}) custom-call(f32[32,1,128]{2,1,0:T(1,128)S(1)} %all_to_all.16.parts_ref, f32[8,4,16,128]{3,2,1,0:T(8,128)S(1)} %get-tuple-element.10.kx_ref, f32[8,4,16,128]{3,2,1,0:T(8,128)S(1)} %get-tuple-element.11.sx_ref), custom_call_target="tpu_custom_call" | custom-call | tf_op jit(solution)/shard_map/pallas_call | solution.py:264
Async XLA Ops:
  0.6 12.1 %copy-start = (bf16[8,4,128,128]{3,2,1,0:T(8,128)(2,1)S(1)}, bf16[8,4,128,128]{3,2,1,0:T(8,128)(2,1)}, u32[]{:S(2)}) copy-start(bf16[8,4,128,128]{3,2,1,0:T(8,128)(2,1)} %mid_ref.1) | copy-start | bytes 3145732
  0.6 50.0 %copy-start.3 = (s32[8]{0:T(128)S(1)}, s32[8]{0:T(128)}, u32[]{:S(2)}) copy-start(s32[8]{0:T(128)} %counts_ref.1) | copy-start | bytes 100
  0.7 49.9 %copy-start.1 = (s32[8,16]{1,0:T(8,128)S(1)}, s32[8,16]{1,0:T(8,128)}, u32[]{:S(2)}) copy-start(s32[8,16]{1,0:T(8,128)} %columns_ref.1) | copy-start | bytes 1540
  0.7 49.9 %copy-start.2 = (f32[8,16]{1,0:T(8,128)S(1)}, f32[8,16]{1,0:T(8,128)}, u32[]{:S(2)}) copy-start(f32[8,16]{1,0:T(8,128)} %onsite_ref.1) | copy-start | bytes 1540
  2.9 47.7 %all-to-all-start = ((bf16[8,2,8,2,16,128]{5,4,3,2,1,0:T(8,128)(2,1)}), bf16[8,2,8,2,16,128]{5,4,3,2,1,0:T(8,128)(2,1)S(1)}, u32[]{:S(2)}, u32[]{:S(2)}) async-start(bf16[8,2,8,2,16,128]{5,4,3,2,1,0:T(8,128)(2,1)} %shard_map.77), calls=%async_computation | async-start | bytes 2097152 | tf_op jit(solution)/shard_map/all_to_all | solution.py:225
  12.8 37.8 %collective-permute-start = (bf16[8,4,128,128]{3,2,1,0:T(8,128)(2,1)S(1)}, bf16[8,4,128,128]{3,2,1,0:T(8,128)(2,1)}, u32[]{:S(2)}, u32[]{:S(2)}) collective-permute-start(bf16[8,4,128,128]{3,2,1,0:T(8,128)(2,1)S(1)} %copy-done), channel_id=1, source_target_pairs={{0,8},{8,16},{16,24},{24,32},{32,40},{40,48},{48,56},{56,64},{64,7... | collective-permute-start | bytes 3145736 | tf_op jit(solution)/shard_map/ppermute | solution.py:208
  16.8 36.3 %collective-permute-start.1 = (bf16[8,4,128,128]{3,2,1,0:T(8,128)(2,1)S(1)}, bf16[8,4,128,128]{3,2,1,0:T(8,128)(2,1)S(1)}, u32[]{:S(2)}, u32[]{:S(2)}) collective-permute-start(bf16[8,4,128,128]{3,2,1,0:T(8,128)(2,1)S(1)} %copy-done), channel_id=1, source_target_pairs={{8,0},{16,8},{24,16},{32,24},{40,32},{48,40},{56,48},{64,56},{72,6... | collective-permute-start | bytes 3145736 | tf_op jit(solution)/shard_map/ppermute | solution.py:209

commit v6 on v4

--- a/solution.py
+++ b/solution.py
@@ -169,7 +169,7 @@
 
 def sum_phases(rows, cols, layers):
     lines = [
-        led([row * cols + c for row in (x, x + 1) for c in range(cols)], x * cols + cols // 2 + 1)
+        led([row * cols + c for row in (x, x + 1) for c in range(cols)], (x + 1) * cols + cols // 2 + 1)
         for x in range(0, rows, 2)
     ]
     planes = [

time: 80.4 us -> 80.1 us (level)
  no operation moved by 1% of the time
where the time goes in v6:
time: 80.1 us; the launch traced here: 79.3 us
  starting transfers between devices  26.9 us (34%)
  blocking collectives  24.3 us (30%)
  waiting for transfers between devices  20.7 us (26%)
  Pallas kernels  6.56 us (8%)
    all_to_all x2, blocking collectives, per_device(): lax.all_to_all(stat, axes, 0, 0, axis_index_groups=groups, tiled=True)  24.3 us
    ppermute x1, waiting for transfers between devices, per_device(): low = lax.ppermute(vectors[rows_blk - REACH:], ('row', 'col'), forward)  20.7 us
    ppermute x1, starting transfers between devices, per_device(): high = lax.ppermute(vectors[:REACH], ('row', 'col'), backward)  13.1 us
    all_to_all x1, starting transfers between devices, per_device(): lax.all_to_all(send, 'state', 0, 0, axis_index_groups=[order], tiled=True)  9.84 us
    ppermute x1, starting transfers between devices, per_device(): low = lax.ppermute(vectors[rows_blk - REACH:], ('row', 'col'), forward)  3.99 us
    pallas_call x1, Pallas kernels, per_device(): pl.pallas_call(functools.partial(early_kernel, states, order), out_shape=...  2.4 us
    pallas_call x1, Pallas kernels, per_device(): pl.pallas_call(functools.partial(send_kernel, order), out_shape=jax.Shape...  2.24 us
  transfers between devices with their start and end apart: 3, of which 1 were waited for; matrix products, arithmetic and copies ran while one was open for 0% of the time, Pallas kernels for 3%

profile of v6, /device:TPU:1, one launch (start us, length us, event | category | flops | bytes accessed | tf_op | source)
XLA Modules:
  0.0 79.3 jit_solution(16080602712629599534)
XLA Ops:
  0.6 0.0 copy-start
  0.6 0.0 copy-start.3
  0.7 0.0 copy-start.1
  0.7 0.0 copy-start.2
  0.7 2.2 %shard_map.77 = bf16[8,2,8,2,16,128]{5,4,3,2,1,0:T(8,128)(2,1)} custom-call(bf16[8,2,128,128]{3,2,1,0:T(8,128)(2,1)} %k_ref.1, bf16[8,2,128,128]{3,2,1,0:T(8,128)(2,1)} %s_ref.1), custom_call_target="tpu_custom_call" | custom-call | tf_op jit(solution)/shard_map/pallas_call | solution.py:202
  2.9 9.8 %all-to-all-start = ((bf16[8,2,8,2,16,128]{5,4,3,2,1,0:T(8,128)(2,1)}), bf16[8,2,8,2,16,128]{5,4,3,2,1,0:T(8,128)(2,1)S(1)}, u32[]{:S(2)}, u32[]{:S(2)}) async-start(bf16[8,2,8,2,16,128]{5,4,3,2,1,0:T(8,128)(2,1)} %shard_map.77), calls=%async_computation | async-start | bytes 2097152 | tf_op jit(solution)/shard_map/all_to_all | solution.py:214
  12.8 0.0 copy-done
  12.8 4.0 %collective-permute-start = (bf16[8,4,128,128]{3,2,1,0:T(8,128)(2,1)S(1)}, bf16[8,4,128,128]{3,2,1,0:T(8,128)(2,1)}, u32[]{:S(2)}, u32[]{:S(2)}) collective-permute-start(bf16[8,4,128,128]{3,2,1,0:T(8,128)(2,1)S(1)} %copy-done), channel_id=1, source_target_pairs={{0,8},{8,16},{16,24},{24,32},{32,40},{40,48},{48,56},{56,64},{64,7... | collective-permute-start | bytes 3145736 | tf_op jit(solution)/shard_map/ppermute | solution.py:197
  16.8 13.1 %collective-permute-start.1 = (bf16[8,4,128,128]{3,2,1,0:T(8,128)(2,1)S(1)}, bf16[8,4,128,128]{3,2,1,0:T(8,128)(2,1)S(1)}, u32[]{:S(2)}, u32[]{:S(2)}) collective-permute-start(bf16[8,4,128,128]{3,2,1,0:T(8,128)(2,1)S(1)} %copy-done), channel_id=1, source_target_pairs={{8,0},{16,8},{24,16},{32,24},{40,32},{48,40},{56,48},{64,56},{72,6... | collective-permute-start | bytes 3145736 | tf_op jit(solution)/shard_map/ppermute | solution.py:198
  29.9 0.1 pad_add_fusion.spot_ref
  29.9 20.7 %collective-permute-done.low_ref = bf16[8,4,128,128]{3,2,1,0:T(8,128)(2,1)} collective-permute-done((bf16[8,4,128,128]{3,2,1,0:T(8,128)(2,1)S(1)}, bf16[8,4,128,128]{3,2,1,0:T(8,128)(2,1)}, u32[]{:S(2)}, u32[]{:S(2)}) %collective-permute-start) | collective-permute-done | bytes 1048608 | tf_op jit(solution)/shard_map/ppermute | solution.py:197
  50.6 0.0 all-to-all-done.tiles_ref
  50.6 0.0 copy-done.3
  50.6 0.0 copy-done.1
  50.6 0.0 copy-done.2
  50.6 2.4 %shard_map.78 = (f32[256,512]{1,0:T(8,128)S(1)}, bf16[256,3200]{1,0:T(8,128)(2,1)S(1)}) custom-call(s32[2]{0:T(128)S(1)} %pad_add_fusion.spot_ref, s32[8,16]{1,0:T(8,128)S(1)} %copy-done.1, s32[8]{0:T(128)S(1)} %copy-done.3, bf16[8,2,8,2,16,128]{5,4,3,2,1,0:T(8,128)(2,1)S(1)} %all-to-all-done.tiles_ref, ...), custom_call_target="tpu_custom_call" | custom-call | tf_op jit(solution)/shard_map/pallas_call | solution.py:220
  53.0 0.0 collective-permute-done.1.high_ref
  53.0 0.8 %shard_map.79 = (f32[8,4,16,128]{3,2,1,0:T(8,128)S(1)}, f32[8,4,16,128]{3,2,1,0:T(8,128)S(1)}, f32[24,1,128]{2,1,0:T(1,128)S(1)}) custom-call(f32[256,512]{1,0:T(8,128)S(1)} %get-tuple-element.7.total_ref, bf16[256,3200]{1,0:T(8,128)(2,1)S(1)} %get-tuple-element.8.oper_ref, bf16[8,4,128,128]{3,2,1,0:T(8,128)(2,1)S(1)} %collective-permute-done.1.high_ref), custom_call_target="tpu_custom_call" | custom-call | tf_op jit(solution)/shard_map/pallas_call | solution.py:234
  53.8 12.3 %all_to_all.15.parts_ref = f32[24,1,128]{2,1,0:T(1,128)S(1)} all-to-all(f32[24,1,128]{2,1,0:T(1,128)S(1)} %get-tuple-element.9), channel_id=1, replica_groups={{152,0,8,16,24,32,40,48,56,64,72,80,88,96,104,112,120,128,136,144,160,1..., dimensions={0} | all-to-all | bytes 24576 | tf_op jit(solution)/shard_map/all_to_all | solution.py:243
  66.1 0.2 shard_map.80
  66.3 12.0 %all_to_all.16.parts_ref = f32[32,1,128]{2,1,0:T(1,128)S(1)} all-to-all(f32[32,1,128]{2,1,0:T(1,128)S(1)} %shard_map.80), channel_id=1, replica_groups={{580,0,1,2,3,4,5,6,7,192,193,194,195,196,197,198,199,384,385,386,387,38..., dimensions={0} | all-to-all | bytes 32768 | tf_op jit(solution)/shard_map/all_to_all | solution.py:252
  78.3 0.9 %shard_map.81 = (f32[8,4,16,128]{3,2,1,0:T(8,128)}, f32[4]{0:T(128)}) custom-call(f32[32,1,128]{2,1,0:T(1,128)S(1)} %all_to_all.16.parts_ref, f32[8,4,16,128]{3,2,1,0:T(8,128)S(1)} %get-tuple-element.10.kx_ref, f32[8,4,16,128]{3,2,1,0:T(8,128)S(1)} %get-tuple-element.11.sx_ref), custom_call_target="tpu_custom_call" | custom-call | tf_op jit(solution)/shard_map/pallas_call | solution.py:253
Async XLA Ops:
  0.6 12.1 %copy-start = (bf16[8,4,128,128]{3,2,1,0:T(8,128)(2,1)S(1)}, bf16[8,4,128,128]{3,2,1,0:T(8,128)(2,1)}, u32[]{:S(2)}) copy-start(bf16[8,4,128,128]{3,2,1,0:T(8,128)(2,1)} %mid_ref.1) | copy-start | bytes 3145732
  0.6 50.0 %copy-start.3 = (s32[8]{0:T(128)S(1)}, s32[8]{0:T(128)}, u32[]{:S(2)}) copy-start(s32[8]{0:T(128)} %counts_ref.1) | copy-start | bytes 100
  0.7 49.9 %copy-start.1 = (s32[8,16]{1,0:T(8,128)S(1)}, s32[8,16]{1,0:T(8,128)}, u32[]{:S(2)}) copy-start(s32[8,16]{1,0:T(8,128)} %columns_ref.1) | copy-start | bytes 1540
  0.7 49.9 %copy-start.2 = (f32[8,16]{1,0:T(8,128)S(1)}, f32[8,16]{1,0:T(8,128)}, u32[]{:S(2)}) copy-start(f32[8,16]{1,0:T(8,128)} %onsite_ref.1) | copy-start | bytes 1540
  2.9 47.7 %all-to-all-start = ((bf16[8,2,8,2,16,128]{5,4,3,2,1,0:T(8,128)(2,1)}), bf16[8,2,8,2,16,128]{5,4,3,2,1,0:T(8,128)(2,1)S(1)}, u32[]{:S(2)}, u32[]{:S(2)}) async-start(bf16[8,2,8,2,16,128]{5,4,3,2,1,0:T(8,128)(2,1)} %shard_map.77), calls=%async_computation | async-start | bytes 2097152 | tf_op jit(solution)/shard_map/all_to_all | solution.py:214
  12.8 37.8 %collective-permute-start = (bf16[8,4,128,128]{3,2,1,0:T(8,128)(2,1)S(1)}, bf16[8,4,128,128]{3,2,1,0:T(8,128)(2,1)}, u32[]{:S(2)}, u32[]{:S(2)}) collective-permute-start(bf16[8,4,128,128]{3,2,1,0:T(8,128)(2,1)S(1)} %copy-done), channel_id=1, source_target_pairs={{0,8},{8,16},{16,24},{24,32},{32,40},{40,48},{48,56},{56,64},{64,7... | collective-permute-start | bytes 3145736 | tf_op jit(solution)/shard_map/ppermute | solution.py:197
  16.8 36.3 %collective-permute-start.1 = (bf16[8,4,128,128]{3,2,1,0:T(8,128)(2,1)S(1)}, bf16[8,4,128,128]{3,2,1,0:T(8,128)(2,1)S(1)}, u32[]{:S(2)}, u32[]{:S(2)}) collective-permute-start(bf16[8,4,128,128]{3,2,1,0:T(8,128)(2,1)S(1)} %copy-done), channel_id=1, source_target_pairs={{8,0},{16,8},{24,16},{32,24},{40,32},{48,40},{56,48},{64,56},{72,6... | collective-permute-start | bytes 3145736 | tf_op jit(solution)/shard_map/ppermute | solution.py:198
